TPU v7x, 128 devices: a whole 4x4x4 slice. The times are simulated.
128 devices in a mesh: row: 8 (over z, core), col: 16 (over y, x).
Axes of the slice: x: 4, y: 4, z: 4, core: 2. Of those that a mesh axis runs over, the one named last changes fastest.
Arguments:
- child_blocks: float32 [256, 64, 3072], P(('row', 'col'))
- home_child: int32 [256], P(('row', 'col')), may hold values from 0 to 255, each once
- col_tiles: int32 [256, 12], replicated, may hold values from 0 to 31, as said below
- tile_owner: int32 [32], replicated, may hold values from 0 to 31, each once
Outputs:
- r_rows: float32 [1024, 8192], P(None, 'col')
Inputs may be any that keep to these rules, and one draw needn't show every extreme that they name: `home_child`: a permutation of the storage slots. `col_tiles`: the tiles of one row are distinct; every row names the tiles 0 to 3; every tile is named by some row. `tile_owner`: a permutation of the tiles.
All inputs are finite; a program needn't handle non-finite values.
Results may differ from a plain program's by a relative error of at most 0.00018.
Values sent between devices are 32-bit elements; how exact they have to be, the bound alone decides.
A program may use at most 192 MiB of HBM per device.

v0:
```python
import jax
import jax.numpy as jnp
from jax import lax
from jax.sharding import PartitionSpec as P

TILE_WIDTH = 256
FRONT_COLS = 8192
CHILD_TILES = 12
CHILD_ROWS = 64
PANELS = 4


def broadcast(x, axis, root):
    mine = lax.axis_index(axis) == root
    return lax.psum(jnp.where(mine, x, jnp.zeros_like(x)), axis)


def storage_positions(home_child, col_tiles, tile_owner):
    count = col_tiles.shape[0]
    tiles_all = tile_owner.shape[0]
    picked = home_child[:, None] == jnp.arange(count, dtype=jnp.int32)[None, :]
    child_tiles = jnp.sum(jnp.where(picked[:, :, None], col_tiles[None, :, :], 0), axis=1)
    matches = child_tiles[:, :, None] == jnp.arange(tiles_all, dtype=jnp.int32)[None, None, :]
    return jnp.sum(jnp.where(matches, tile_owner[None, None, :], 0), axis=2)


def body(child_blocks, home_child, col_tiles, tile_owner):
    highest = lax.Precision.HIGHEST
    col_count = lax.axis_size("col")
    local_cols = FRONT_COLS // col_count
    held = local_cols // TILE_WIDTH
    my_col = lax.axis_index("col")
    first_held = my_col * held
    position = storage_positions(home_child, col_tiles, tile_owner)
    piece_blocks = lax.all_gather(child_blocks, "col", axis=0, tiled=True)
    piece_slots = lax.all_gather(position, "col", axis=0, tiled=True)
    count = piece_blocks.shape[0]
    local_tile = piece_slots - first_held
    mine = (local_tile[:, :, None] == jnp.arange(held, dtype=jnp.int32)[None, None, :]).astype(
        jnp.float32
    )
    shaped = piece_blocks.reshape(count, CHILD_ROWS, CHILD_TILES, TILE_WIDTH)
    placed = jnp.einsum("nrjc,njk->nrkc", shaped, mine, precision=highest)
    placed = placed.reshape(count * CHILD_ROWS, local_cols)
    front = placed
    identity = jnp.eye(TILE_WIDTH, dtype=jnp.float32)
    results = []
    for step in range(PANELS):
        stored_at = tile_owner[step]
        holder = stored_at // held
        offset = (stored_at - holder * held) * TILE_WIDTH
        is_holder = holder == my_col
        panel = lax.dynamic_slice_in_dim(front, offset, TILE_WIDTH, 1)
        panel = jnp.where(is_holder, panel, 0.0)
        gram_part = jnp.dot(panel.T, panel, precision=highest, preferred_element_type=jnp.float32)
        gram = lax.psum(gram_part, "row")
        gram = gram + jnp.where(is_holder, 0.0, identity)
        lower = jnp.linalg.cholesky(gram)
        basis = jax.scipy.linalg.solve_triangular(lower, panel.T, lower=True).T
        basis = broadcast(basis, "col", holder)
        local_proj = jnp.dot(basis.T, front, precision=highest, preferred_element_type=jnp.float32)
        projected = lax.psum(local_proj, "row")
        front = front - jnp.dot(
            basis, projected, precision=highest, preferred_element_type=jnp.float32
        )
        results.append(projected)
    stacked = jnp.concatenate(results, axis=0)
    return stacked


def solution(mesh):
    return jax.shard_map(
        body,
        mesh=mesh,
        in_specs=(P(("row", "col"), None, None), P(("row", "col")), P(), P()),
        out_specs=P(None, "col"),
        check_vma=False,
    )
```

profile of v0, /device:TPU:1, one launch (start us, length us, event | category | flops | bytes accessed | tf_op | source)
XLA Modules:
  0.0 1399.5 jit_solution(9033464079594677227)
XLA Ops:
  14.9 20.2 %all-gather = s32[16,2,12]{2,1,0:T(2,128)S(1)} all-gather(s32[1,2,12]{2,1,0:T(2,128)S(1)} %bitcast.177), channel_id=1, replica_groups=mesh['row'=8,'col'=16] {'col'}, dimensions={0}, use_global_device_ids=true | all-gather | bytes 1632 | tf_op jit(solution)/shard_map/all_gather | solution.py:36
  35.0 131.8 %all-gather.3.cloned.1.call-done = f32[32,64,3072]{2,1,0:T(8,128)} async-done(((f32[2,64,3072]{2,1,0:T(8,128)}), f32[32,64,3072]{2,1,0:T(8,128)}) %all-gather.3.cloned.1.call-update) | async-done | bytes 25165840 | tf_op jit(solution)/shard_map/all_gather | solution.py:35
  166.8 30.4 %reshape.46 = f32[32,64,12,256]{3,2,1,0:T(8,128)} reshape(f32[32,64,3072]{2,1,0:T(8,128)} %all-gather.3.cloned.1.call-done) | data formatting | bytes 50331648 | tf_op jit(solution)/shard_map/reshape | solution.py:42
  197.2 17.6 %fusion.56 = f32[32,2,64,256]{3,1,2,0:T(2,128)S(1)} fusion(f32[32,64,12,256]{3,2,1,0:T(8,128)} %reshape.46, s32[32,12]{1,0:T(8,128)S(1)} %bitcast.175), kind=kOutput, calls=%fused_computation.120 | convolution fusion | flops 150995712 | bytes 29361664 | tf_op jit(solution)/shard_map/nrjc,njk->nrkc/dot_general | solution.py:43
  229.5 55.8 %all-reduce.14.cloned.1.call-done = f32[256,256]{0,1:T(8,128)} async-done(((f32[256,256]{0,1:T(8,128)}), f32[256,256]{0,1:T(8,128)}) %all-reduce.14.cloned.1.call-update) | async-done | bytes 262160 | tf_op jit(solution)/shard_map/psum | solution.py:56
  309.6 11.7 cholesky.231
  327.5 19.7 %custom-call.18 = f32[2,128,128]{1,2,0:T(8,128)S(1)} custom-call(f32[2,128,128]{2,1,0:T(8,128)S(1)} %get-tuple-element.33), custom_call_target="InvertDiagBlocksLowerTriangular" | custom-call | tf_op jit(solution)/shard_map/jit(_solve_triangular)/triangular_solve | solution.py:59
  351.9 90.1 %all-reduce.16.cloned.1.call-done = f32[2048,256]{0,1:T(8,128)} async-done(((f32[2048,256]{0,1:T(8,128)}), f32[2048,256]{0,1:T(8,128)}) %all-reduce.16.cloned.1.call-update) | async-done | bytes 2097168 | tf_op jit(solution)/shard_map/psum | solution.py:15
  452.7 56.3 %all-reduce.18.cloned.1.call-done = f32[256,512]{1,0:T(8,128)} async-done(((f32[256,512]{1,0:T(8,128)}), f32[256,512]{1,0:T(8,128)}) %all-reduce.18.cloned.1.call-update) | async-done | bytes 524304 | tf_op jit(solution)/shard_map/psum | solution.py:62
  521.2 57.3 %all-reduce.20.cloned.1.call-done = f32[256,256]{0,1:T(8,128)} async-done(((f32[256,256]{0,1:T(8,128)}), f32[256,256]{0,1:T(8,128)}) %all-reduce.20.cloned.1.call-update) | async-done | bytes 262160 | tf_op jit(solution)/shard_map/psum | solution.py:56
  602.7 11.7 cholesky.265
  621.2 19.7 %custom-call.20 = f32[2,128,128]{1,2,0:T(8,128)S(1)} custom-call(f32[2,128,128]{2,1,0:T(8,128)S(1)} %get-tuple-element.34), custom_call_target="InvertDiagBlocksLowerTriangular" | custom-call | tf_op jit(solution)/shard_map/jit(_solve_triangular)/triangular_solve | solution.py:59
  645.6 90.1 %all-reduce.22.cloned.1.call-done = f32[2048,256]{0,1:T(8,128)} async-done(((f32[2048,256]{0,1:T(8,128)}), f32[2048,256]{0,1:T(8,128)}) %all-reduce.22.cloned.1.call-update) | async-done | bytes 2097168 | tf_op jit(solution)/shard_map/psum | solution.py:15
  746.4 56.3 %all-reduce.24.cloned.1.call-done = f32[256,512]{1,0:T(8,128)} async-done(((f32[256,512]{1,0:T(8,128)}), f32[256,512]{1,0:T(8,128)}) %all-reduce.24.cloned.1.call-update) | async-done | bytes 524304 | tf_op jit(solution)/shard_map/psum | solution.py:62
  815.2 57.0 %all-reduce.26.cloned.1.call-done = f32[256,256]{0,1:T(8,128)} async-done(((f32[256,256]{0,1:T(8,128)}), f32[256,256]{0,1:T(8,128)}) %all-reduce.26.cloned.1.call-update) | async-done | bytes 262160 | tf_op jit(solution)/shard_map/psum | solution.py:56
  896.4 11.7 cholesky.299
  914.9 19.7 %custom-call.22 = f32[2,128,128]{1,2,0:T(8,128)S(1)} custom-call(f32[2,128,128]{2,1,0:T(8,128)S(1)} %get-tuple-element.35), custom_call_target="InvertDiagBlocksLowerTriangular" | custom-call | tf_op jit(solution)/shard_map/jit(_solve_triangular)/triangular_solve | solution.py:59
  939.3 90.1 %all-reduce.28.cloned.1.call-done = f32[2048,256]{0,1:T(8,128)} async-done(((f32[2048,256]{0,1:T(8,128)}), f32[2048,256]{0,1:T(8,128)}) %all-reduce.28.cloned.1.call-update) | async-done | bytes 2097168 | tf_op jit(solution)/shard_map/psum | solution.py:15
  1039.7 56.7 %all-reduce.30.cloned.1.call-done = f32[256,512]{1,0:T(8,128)} async-done(((f32[256,512]{1,0:T(8,128)}), f32[256,512]{1,0:T(8,128)}) %all-reduce.30.cloned.1.call-update) | async-done | bytes 524304 | tf_op jit(solution)/shard_map/psum | solution.py:62
  1108.7 57.3 %all-reduce.32.cloned.1.call-done = f32[256,256]{0,1:T(8,128)} async-done(((f32[256,256]{0,1:T(8,128)}), f32[256,256]{0,1:T(8,128)}) %all-reduce.32.cloned.1.call-update) | async-done | bytes 262160 | tf_op jit(solution)/shard_map/psum | solution.py:56
  1190.2 11.7 cholesky.333
  1208.7 19.7 %custom-call.24 = f32[2,128,128]{1,2,0:T(8,128)S(1)} custom-call(f32[2,128,128]{2,1,0:T(8,128)S(1)} %get-tuple-element.36), custom_call_target="InvertDiagBlocksLowerTriangular" | custom-call | tf_op jit(solution)/shard_map/jit(_solve_triangular)/triangular_solve | solution.py:59
  1233.1 90.0 %all-reduce.34.cloned.1.call-done = f32[2048,256]{0,1:T(8,128)} async-done(((f32[2048,256]{0,1:T(8,128)}), f32[2048,256]{0,1:T(8,128)}) %all-reduce.34.cloned.1.call-update) | async-done | bytes 2097168 | tf_op jit(solution)/shard_map/psum | solution.py:15
  1330.5 59.5 %all-reduce.36.cloned.1.call-done = f32[256,512]{1,0:T(8,128)} async-done(((f32[256,512]{1,0:T(8,128)}), f32[256,512]{1,0:T(8,128)}) %all-reduce.36.cloned.1.call-update) | async-done | bytes 524304 | tf_op jit(solution)/shard_map/psum | solution.py:62
  (173 shorter events, 241.3 us)
Async XLA Ops:
  6.5 160.3 %all-gather.3.cloned.1.call-start = ((), (), s32[]{:S(2)}) async-start(), calls=%async_computation | async-start | bytes 26738688 | tf_op jit(solution)/shard_map/all_gather | solution.py:35
  7.3 278.1 %all-reduce.14.cloned.1.call-start = ((), (), s32[]{:S(2)}) async-start(), calls=%async_computation.1 | async-start | bytes 524288 | tf_op jit(solution)/shard_map/psum | solution.py:56
  227.5 214.4 %all-reduce.16.cloned.1.call-start = ((), (), s32[]{:S(2)}) async-start(), calls=%async_computation.2 | async-start | bytes 4194304 | tf_op jit(solution)/shard_map/psum | solution.py:15
  351.9 157.1 %all-reduce.18.cloned.1.call-start = ((), (), s32[]{:S(2)}) async-start(), calls=%async_computation.3 | async-start | bytes 1048576 | tf_op jit(solution)/shard_map/psum | solution.py:62
  442.0 67.0 %copy-start.4 = (f32[2048,256]{0,1:T(8,128)S(1)}, f32[2048,256]{0,1:T(8,128)}, u32[]{:S(2)}) copy-start(f32[2048,256]{0,1:T(8,128)} %all-reduce.16.cloned.1.call-done) | copy-start | bytes 6291460
  449.5 129.1 %all-reduce.20.cloned.1.call-start = ((), (), s32[]{:S(2)}) async-start(), calls=%async_computation.4 | async-start | bytes 524288 | tf_op jit(solution)/shard_map/psum | solution.py:56
  514.7 1.9 copy-start.1
  519.3 216.4 %all-reduce.22.cloned.1.call-start = ((), (), s32[]{:S(2)}) async-start(), calls=%async_computation.5 | async-start | bytes 4194304 | tf_op jit(solution)/shard_map/psum | solution.py:15
  645.6 157.2 %all-reduce.24.cloned.1.call-start = ((), (), s32[]{:S(2)}) async-start(), calls=%async_computation.6 | async-start | bytes 1048576 | tf_op jit(solution)/shard_map/psum | solution.py:62
  735.7 67.0 %copy-start.5 = (f32[2048,256]{0,1:T(8,128)S(1)}, f32[2048,256]{0,1:T(8,128)}, u32[]{:S(2)}) copy-start(f32[2048,256]{0,1:T(8,128)} %all-reduce.22.cloned.1.call-done) | copy-start | bytes 6291460
  743.2 129.1 %all-reduce.26.cloned.1.call-start = ((), (), s32[]{:S(2)}) async-start(), calls=%async_computation.7 | async-start | bytes 524288 | tf_op jit(solution)/shard_map/psum | solution.py:56
  808.4 1.9 copy-start
  813.0 216.4 %all-reduce.28.cloned.1.call-start = ((), (), s32[]{:S(2)}) async-start(), calls=%async_computation.8 | async-start | bytes 4194304 | tf_op jit(solution)/shard_map/psum | solution.py:15
  939.2 157.2 %all-reduce.30.cloned.1.call-start = ((), (), s32[]{:S(2)}) async-start(), calls=%async_computation.9 | async-start | bytes 1048576 | tf_op jit(solution)/shard_map/psum | solution.py:62
  1029.4 67.0 %copy-start.3 = (f32[2048,256]{0,1:T(8,128)S(1)}, f32[2048,256]{0,1:T(8,128)}, u32[]{:S(2)}) copy-start(f32[2048,256]{0,1:T(8,128)} %all-reduce.28.cloned.1.call-done) | copy-start | bytes 6291460
  1036.9 129.1 %all-reduce.32.cloned.1.call-start = ((), (), s32[]{:S(2)}) async-start(), calls=%async_computation.10 | async-start | bytes 524288 | tf_op jit(solution)/shard_map/psum | solution.py:56
  1102.1 1.9 copy-start.2
  1106.7 216.4 %all-reduce.34.cloned.1.call-start = ((), (), s32[]{:S(2)}) async-start(), calls=%async_computation.11 | async-start | bytes 4194304 | tf_op jit(solution)/shard_map/psum | solution.py:15
  1233.0 157.0 %copy-start.6 = (f32[256,512]{1,0:T(8,128)S(1)}, f32[256,512]{1,0:T(8,128)}, u32[]{:S(2)}) copy-start(f32[256,512]{1,0:T(8,128)} %all-reduce.18.cloned.1.call-done) | copy-start | bytes 1572868
  1233.0 157.0 %copy-start.7 = (f32[256,512]{1,0:T(8,128)S(1)}, f32[256,512]{1,0:T(8,128)}, u32[]{:S(2)}) copy-start(f32[256,512]{1,0:T(8,128)} %all-reduce.24.cloned.1.call-done) | copy-start | bytes 1572868
  1233.1 157.0 %copy-start.8 = (f32[256,512]{1,0:T(8,128)S(1)}, f32[256,512]{1,0:T(8,128)}, u32[]{:S(2)}) copy-start(f32[256,512]{1,0:T(8,128)} %all-reduce.30.cloned.1.call-done) | copy-start | bytes 1572868
  1233.1 157.0 %all-reduce.36.cloned.1.call-start = ((), (), s32[]{:S(2)}) async-start(), calls=%async_computation.12 | async-start | bytes 1048576 | tf_op jit(solution)/shard_map/psum | solution.py:62
Sparse Core Ops, SparseCore 0:
  9.5 157.2 all-gather.2
  227.7 57.6 all-reduce.13
  352.0 89.9 all-reduce.15
  449.6 59.3 all-reduce.17
  519.4 59.0 all-reduce.19
  645.7 89.9 all-reduce.21
  743.3 59.3 all-reduce.23
  813.1 59.0 all-reduce.25
  939.4 89.9 all-reduce.27
  1037.0 59.3 all-reduce.29
  1106.8 59.0 all-reduce.31
  1233.2 89.9 all-reduce.33
  1330.6 59.3 all-reduce.35
where the time goes:
time: 1410 us; the launch traced here: 1400 us
  waiting for transfers between devices  949 us (67%)
  other arithmetic  243 us (17%)
  matrix products  91.5 us (6%)
  local copies, waits for them, and re-layouts  61.7 us (4%)
  between operations  31.7 us (2%)
  blocking collectives  20.2 us (1%)
    psum x4, waiting for transfers between devices, broadcast(): return lax.psum(jnp.where(mine, x, jnp.zeros_like(x)), axis)  360 us
    psum x4, waiting for transfers between devices, body(): projected = lax.psum(local_proj, 'row')  229 us
    psum x4, waiting for transfers between devices, body(): gram = lax.psum(gram_part, 'row')  227 us
    another operation x27, other arithmetic, body(): lower = jnp.linalg.cholesky(gram)  138 us
    all_gather x1, waiting for transfers between devices, body(): piece_blocks = lax.all_gather(child_blocks, 'col', axis=0, tiled=True)  132 us
    another operation x9, other arithmetic, body(): basis = jax.scipy.linalg.solve_triangular(lower, panel.T, lower=True).T  78.8 us
    reshape x1, local copies, waits for them, and re-layouts, body(): shaped = piece_blocks.reshape(count, CHILD_ROWS, CHILD_TILES, TILE_WIDTH)  30.4 us
    dot_general x4, matrix products, body(): jnp.dot(basis.T, front, precision=highest, preferred_element_type=jnp.flo...  29.7 us
  transfers between devices with their start and end apart: 13, of which 13 were waited for; matrix products, arithmetic and copies ran while one was open for 1% of the time, Pallas kernels for 0%

commit v1 on v0

--- a/solution.py
+++ b/solution.py
@@ -1,13 +1,541 @@
 import jax
 import jax.numpy as jnp
 from jax import lax
+from jax.experimental import pallas as pl
+from jax.experimental.pallas import tpu as pltpu
 from jax.sharding import PartitionSpec as P
 
-TILE_WIDTH = 256
+T = 256
+TILES = 32
+CT = 12
+ROWS = 64
 FRONT_COLS = 8192
-CHILD_TILES = 12
-CHILD_ROWS = 64
 PANELS = 4
+OWN = 2
+REST = CT - PANELS
+H = 2
+HW = T // H
+NEWTON = 4
+RESIDUAL = 1e-5
+SHARE = 0.1
+F32 = jnp.float32
+BF = jnp.bfloat16
+MESH = pl.DeviceIdType.MESH
+BLOCKS = [(q, r) for q in range(PANELS) for r in range(q, PANELS)]
+BLK = {qr: i for i, qr in enumerate(BLOCKS)}
+GROWS = len(BLOCKS) * T
+GHALF = GROWS // 2
+GQ = GHALF // 2
+GC = GQ // 4
+GS = GC // 4
+
+
+def split(x):
+    hi = x.astype(BF)
+    lo = (x - hi.astype(F32)).astype(BF)
+    return hi, lo
+
+
+def dg(a, b, ca, cb):
+    return lax.dot_general(a, b, (((ca,), (cb,)), ((), ())), preferred_element_type=F32)
+
+
+def dot3(a, b, ca=1, cb=0):
+    ah, al = a
+    bh, bl = b
+    return dg(ah, bh, ca, cb) + (dg(ah, bl, ca, cb) + dg(al, bh, ca, cb))
+
+
+def sort_kernel(home_ref, tiles_ref, owner_ref, blocks_ref, panels_ref, packed_ref, table_ref):
+    lane = lax.broadcasted_iota(jnp.int32, (8, 128), 1)
+    sub = lax.broadcasted_iota(jnp.int32, (8, 128), 0)
+    table = jnp.full((8, 128), REST, jnp.int32)
+    place = []
+    for c in range(OWN):
+        home = home_ref[c]
+        panel_at = [jnp.int32(0)] * PANELS
+        rest_at = [jnp.int32(0)] * REST
+        count = jnp.int32(0)
+        for j in range(CT):
+            t = tiles_ref[home, j]
+            p = owner_ref[t]
+            rest = t >= PANELS
+            for m in range(PANELS):
+                panel_at[m] = jnp.where(t == m, j, panel_at[m])
+            for i in range(min(j + 1, REST)):
+                rest_at[i] = jnp.where(jnp.logical_and(rest, count == i), j, rest_at[i])
+            table = jnp.where(
+                jnp.logical_and(jnp.logical_and(lane == p, sub == c), rest), count, table)
+            count = count + rest.astype(jnp.int32)
+        place.append((panel_at, rest_at))
+    table_ref[...] = table
+    for c in range(OWN):
+        for m in range(PANELS):
+            at = pl.multiple_of(place[c][0][m] * T, T)
+            panels_ref[m, c * ROWS:(c + 1) * ROWS, :] = blocks_ref[c, :, pl.ds(at, T)]
+        for i in range(REST):
+            at = pl.multiple_of(place[c][1][i] * T, T)
+            got = blocks_ref[c, :, pl.ds(at, T)]
+            for h in range(H):
+                packed_ref[h, c * ROWS:(c + 1) * ROWS, i * HW:(i + 1) * HW] = (
+                    got[:, h * HW:(h + 1) * HW])
+
+
+def kernel(
+    owner_ref, pown, packed_ref, table_ref,
+    out_ref, good_ref,
+    ag, pg, tab, tab_s, agh, agl, pth, ptl, bh, bl, sp,
+    ra, rb, sa, sb, ra2, rb2, sfull,
+    gbuf, grc, ga, gb, gsa, gsb, ga2, gb2, gza, gzb,
+    wref, wh_ref, wl_ref, cw, uth, utl, rp,
+    xsem_s, xsem_r, lsem,
+):
+    row = lax.axis_index("row")
+    col = lax.axis_index("col")
+    z = row // 2
+    k = row % 2
+    y = col // 4
+    x = col % 4
+    sib = (z * 2 + (1 - k), col)
+
+    def zp(d):
+        return (lax.rem(z + d, 4) * 2 + k, col)
+
+    def xp(d):
+        return (row, y * 4 + lax.rem(x + d, 4))
+
+    def yp(d):
+        return (row, lax.rem(y + d, 4) * 4 + x)
+
+    barrier = pltpu.get_barrier_semaphore()
+    partners = [sib] + [f(d) for f in (zp, xp, yp) for d in (1, 2, 3)]
+    for dev in partners:
+        pl.semaphore_signal(barrier, inc=1, device_id=dev, device_id_type=MESH)
+
+    counter = [0]
+
+    def rcopy(src, dst, dev):
+        i = counter[0]
+        counter[0] += 1
+        return pltpu.make_async_remote_copy(
+            src_ref=src, dst_ref=dst, send_sem=xsem_s.at[i], recv_sem=xsem_r.at[i],
+            device_id=dev, device_id_type=MESH,
+        )
+
+    sends = []
+    left_early = []
+
+    def go(copy):
+        copy.start()
+        sends.append(copy)
+        return copy
+
+    pg[z, k] = pown[z]
+    tab[z, k] = table_ref[...]
+    for h in range(H):
+        ag[z, k, h] = packed_ref[h]
+    pl.semaphore_wait(barrier, len(partners))
+
+    pz, tz = [], []
+    for d in (1, 2, 3):
+        pz.append(go(rcopy(pown.at[lax.rem(z + d, 4)], pg.at[z, k], zp(d))))
+        tz.append(go(rcopy(tab.at[z, k], tab.at[z, k], zp(d))))
+    psib = [go(rcopy(pown.at[z], pg.at[z, k], sib))]
+    tsib = [go(rcopy(tab.at[z, k], tab.at[z, k], sib))]
+
+    def rows(c):
+        return pl.ds(c * ROWS, ROWS)
+
+    ar, al_, asib = {}, {}, {}
+
+    def start_a(h):
+        for c in range(OWN):
+            me = ag.at[z, k, h, rows(c)]
+            ar[h, c] = go(rcopy(me, me, zp(1)))
+            other = ag.at[z, k, h, rows(1 - c)]
+            al_[h, 1 - c] = go(rcopy(other, other, zp(3)))
+        mine = ag.at[z, k, h]
+        asib[h] = [go(rcopy(mine, mine, sib))]
+
+    start_a(0)
+    fr, fl = {}, {}
+
+    def forward_a(h):
+        left = lax.rem(z + 3, 4)
+        right = lax.rem(z + 1, 4)
+        ar[h, 0].wait_recv()
+        v = ag.at[left, k, h, rows(0)]
+        fr[h] = go(rcopy(v, v, zp(1)))
+        al_[h, 1].wait_recv()
+        v = ag.at[right, k, h, rows(1)]
+        fl[h] = go(rcopy(v, v, zp(3)))
+        ar[h, 1].wait_recv()
+        v = ag.at[left, k, h]
+        asib[h].append(go(rcopy(v, v, sib)))
+        al_[h, 0].wait_recv()
+        v = ag.at[right, k, h]
+        asib[h].append(go(rcopy(v, v, sib)))
+
+    def finish_a(h):
+        far = lax.rem(z + 2, 4)
+        fr[h].wait_recv()
+        fl[h].wait_recv()
+        v = ag.at[far, k, h]
+        asib[h].append(go(rcopy(v, v, sib)))
+
+    def forward_p():
+        for i, d in enumerate((1, 2, 3)):
+            src = lax.rem(z + 4 - d, 4)
+            pz[i].wait_recv()
+            tz[i].wait_recv()
+            v = pg.at[src, k]
+            psib.append(go(rcopy(v, v, sib)))
+            t = tab.at[src, k]
+            tsib.append(go(rcopy(t, t, sib)))
+
+    def gram():
+        halves = [split(pown[m]) for m in range(PANELS)]
+        for i, (q, r) in enumerate(BLOCKS):
+            gbuf[i * T:(i + 1) * T, :] = dot3(halves[q], halves[r], 0, 0)
+
+    gram()
+    gk = pl.multiple_of(k * GHALF, GHALF)
+    go_ = pl.multiple_of((1 - k) * GHALF, GHALF)
+    g0 = go(rcopy(gbuf.at[pl.ds(go_, GHALF)], grc, sib))
+    g0.wait_recv()
+
+    def add_rows(dst, off, n, srcs):
+        step = 160 if n % 160 == 0 else n
+
+        def body(i, carry):
+            o = pl.multiple_of(i * step, 8)
+            acc = dst[pl.ds(off + o, step), :]
+            for s in srcs:
+                acc = acc + s[pl.ds(o, step), :]
+            dst[pl.ds(off + o, step), :] = acc
+            return carry
+
+        lax.fori_loop(0, n // step, body, 0)
+
+    add_rows(gbuf, gk, GHALF, [grc])
+    base_a = gk
+    base_b = pl.multiple_of(gk + GQ, GQ)
+    g1a, g1b = [], []
+    for d in (1, 2, 3):
+        ox = pl.multiple_of(base_a + lax.rem(x + d, 4) * GC, GC)
+        oy = pl.multiple_of(base_b + lax.rem(y + d, 4) * GC, GC)
+        g1a.append(go(rcopy(gbuf.at[pl.ds(ox, GC)], ga.at[d - 1], xp(d))))
+        g1b.append(go(rcopy(gbuf.at[pl.ds(oy, GC)], gb.at[d - 1], yp(d))))
+    forward_p()
+    for c in g1a + g1b:
+        c.wait_recv()
+    my_a = pl.multiple_of(base_a + x * GC, GC)
+    my_b = pl.multiple_of(base_b + y * GC, GC)
+    gsa[...] = gbuf[pl.ds(my_a, GC), :] + ga[0] + ga[1] + ga[2]
+    gsb[...] = gbuf[pl.ds(my_b, GC), :] + gb[0] + gb[1] + gb[2]
+    g2a, g2b = [], []
+    for d in (1, 2, 3):
+        oy = pl.multiple_of(lax.rem(y + d, 4) * GS, GS)
+        ox = pl.multiple_of(lax.rem(x + d, 4) * GS, GS)
+        g2a.append(go(rcopy(gsa.at[pl.ds(oy, GS)], ga2.at[d - 1], yp(d))))
+        g2b.append(go(rcopy(gsb.at[pl.ds(ox, GS)], gb2.at[d - 1], xp(d))))
+    for c in g2a + g2b:
+        c.wait_recv()
+    oya = pl.multiple_of(y * GS, GS)
+    oxb = pl.multiple_of(x * GS, GS)
+    gza[z] = gsa[pl.ds(oya, GS), :] + ga2[0] + ga2[1] + ga2[2]
+    gzb[z] = gsb[pl.ds(oxb, GS), :] + gb2[0] + gb2[1] + gb2[2]
+    g3 = []
+    for d in (1, 2, 3):
+        g3.append(go(rcopy(gza.at[z], gza.at[z], zp(d))))
+        g3.append(go(rcopy(gzb.at[z], gzb.at[z], zp(d))))
+    forward_a(0)
+    for c in g3:
+        c.wait_recv()
+    fa = pl.multiple_of(my_a + y * GS, GS)
+    fb = pl.multiple_of(my_b + x * GS, GS)
+    gfin_a = gza[0] + gza[1] + gza[2] + gza[3]
+    gfin_b = gzb[0] + gzb[1] + gzb[2] + gzb[3]
+    cw[pl.ds(fa, GS), :] = gfin_a
+    cw[pl.ds(fb, GS), :] = gfin_b
+    g4 = []
+    for d in (1, 2, 3):
+        v = cw.at[pl.ds(fa, GS)]
+        g4.append(go(rcopy(v, v, yp(d))))
+        v = cw.at[pl.ds(fb, GS)]
+        g4.append(go(rcopy(v, v, xp(d))))
+    for c in g4:
+        c.wait_recv()
+    g5 = []
+    for d in (1, 2, 3):
+        v = cw.at[pl.ds(my_a, GC)]
+        g5.append(go(rcopy(v, v, xp(d))))
+        v = cw.at[pl.ds(my_b, GC)]
+        g5.append(go(rcopy(v, v, yp(d))))
+    finish_a(0)
+    for c in g5:
+        c.wait_recv()
+    v = cw.at[pl.ds(gk, GHALF)]
+    g6 = go(rcopy(v, v, sib))
+    start_a(1)
+
+    for c in psib + tsib:
+        c.wait_recv()
+    tcopy = pltpu.make_async_copy(tab, tab_s, lsem.at[0])
+    tcopy.start()
+    for i in range(8):
+        hi, lo = split(jnp.transpose(pg[i // 2, i % 2]))
+        pth[:, i * 128:(i + 1) * 128] = hi
+        ptl[:, i * 128:(i + 1) * 128] = lo
+    tcopy.wait()
+    zero = jnp.zeros((8 * 128, HW), BF)
+    agh[REST] = zero
+    agl[REST] = zero
+
+    def products(h):
+        for c in asib[h]:
+            c.wait_recv()
+
+        def conv(i, carry):
+            o = pl.multiple_of(i * 128, 128)
+            hi, lo = split(ag[i // 2, lax.rem(i, 2), h])
+            for t in range(REST):
+                agh[t, pl.ds(o, 128), :] = hi[:, t * HW:(t + 1) * HW]
+                agl[t, pl.ds(o, 128), :] = lo[:, t * HW:(t + 1) * HW]
+            return carry
+
+        lax.fori_loop(0, 8, conv, 0)
+
+        def pair(i, carry):
+            for s in range(2):
+                slot = (2 * i + s) * 2 + k
+                for n in range(16):
+                    at = tab_s[n // 4, (n // 2) % 2, n % 2, slot]
+                    bh[n * ROWS:(n + 1) * ROWS, s * HW:(s + 1) * HW] = (
+                        agh[at, n * ROWS:(n + 1) * ROWS, :])
+                    bl[n * ROWS:(n + 1) * ROWS, s * HW:(s + 1) * HW] = (
+                        agl[at, n * ROWS:(n + 1) * ROWS, :])
+            got = dot3((pth[...], ptl[...]), (bh[...], bl[...]))
+            yy = (2 * i) // 4
+            xx = lax.rem(2 * i, 4)
+            sp[h, yy, xx] = got[:, 0:HW]
+            sp[h, yy, xx + 1] = got[:, HW:]
+            return carry
+
+        lax.fori_loop(0, 8, pair, 0)
+
+    s1, s2, s3 = {}, {}, {}
+
+    def reduce1(h):
+        s1[h] = []
+        for d in (1, 2, 3):
+            s1[h].append(go(rcopy(
+                sp.at[h, :, lax.rem(x + d, 4), pl.ds(0, 128)], ra.at[h, d - 1], xp(d))))
+            s1[h].append(go(rcopy(
+                sp.at[h, lax.rem(y + d, 4), :, pl.ds(128, 128)], rb.at[h, d - 1], yp(d))))
+
+    def reduce2(h):
+        for c in s1[h]:
+            c.wait_recv()
+        for i in range(4):
+            sa[h, i] = sp[h, i, x, 0:128, :] + ra[h, 0, i] + ra[h, 1, i] + ra[h, 2, i]
+            sb[h, i] = sp[h, y, i, 128:256, :] + rb[h, 0, i] + rb[h, 1, i] + rb[h, 2, i]
+        s2[h] = []
+        for d in (1, 2, 3):
+            s2[h].append(go(rcopy(sa.at[h, lax.rem(y + d, 4)], ra2.at[h, d - 1], yp(d))))
+            s2[h].append(go(rcopy(sb.at[h, lax.rem(x + d, 4)], rb2.at[h, d - 1], xp(d))))
+
+    def gather1(h):
+        for c in s2[h]:
+            c.wait_recv()
+        sfull[z, k, h, 0:128, :] = sa[h, y] + ra2[h, 0] + ra2[h, 1] + ra2[h, 2]
+        sfull[z, k, h, 128:256, :] = sb[h, x] + rb2[h, 0] + rb2[h, 1] + rb2[h, 2]
+        v = sfull.at[z, k, h]
+        s3[h] = [go(rcopy(v, v, zp(d))) for d in (1, 2, 3)]
+        s3[h].append(go(rcopy(v, v, sib)))
+
+    def gather2(h):
+        for d in (1, 2, 3):
+            s3[h][d - 1].wait_recv()
+            v = sfull.at[lax.rem(z + 4 - d, 4), k, h]
+            s3[h].append(go(rcopy(v, v, sib)))
+
+    rr = lax.broadcasted_iota(jnp.int32, (T, T), 0)
+    cc = lax.broadcasted_iota(jnp.int32, (T, T), 1)
+    eye = rr == cc
+    phi = jnp.where(eye, 0.5, jnp.where(rr > cc, 1.0, 0.0)).astype(F32)
+    ident = jnp.where(eye, 1.0, 0.0).astype(F32)
+    checks = []
+    lengths = []
+
+    def block(q, r):
+        i = BLK[q, r]
+        return pl.ds(i * T, T)
+
+    def factor(p):
+        if p == 0:
+            for q in range(PANELS):
+                diag = jnp.where(eye, cw[block(q, q), :], 0.0)
+                lengths.append(jnp.sum(diag, axis=0, keepdims=True))
+        c0 = cw[block(p, p), :]
+        diag = jnp.where(eye, c0, 0.0)
+        left = jnp.sum(diag, axis=0, keepdims=True)
+        dr = lax.rsqrt(left)
+        dc = lax.rsqrt(jnp.sum(diag, axis=1, keepdims=True))
+        scaled = c0 * dr * dc
+        sh, sl = split(scaled)
+        n0 = phi * (scaled - ident)
+        wref[...] = ident - n0
+
+        def it(i, carry):
+            w = split(wref[...])
+            t = split(dot3(w, (sh, sl)))
+            e = dot3(t, w, 1, 1) - ident
+            n = phi * e
+            wref[...] = wref[...] - dot3(split(n), w)
+            return jnp.sum(e * e, axis=0, keepdims=True)
+
+        err = lax.fori_loop(0, NEWTON - 1, it, jnp.zeros((1, T), F32))
+        checks.append(jnp.sum(err) < RESIDUAL)
+        checks.append(jnp.min(left - SHARE * lengths[p]) > 0.0)
+        w = wref[...] * dr
+        hi, lo = split(w)
+        wh_ref[p] = hi
+        wl_ref[p] = lo
+        for r in range(p, PANELS):
+            c = split(cw[block(p, r), :])
+            u = dot3((hi, lo), c)
+            rp[r, p] = u
+            if r > p:
+                uh, ul = split(jnp.transpose(u))
+                uth[BLK[p, r]] = uh
+                utl[BLK[p, r]] = ul
+        for q in range(p + 1, PANELS):
+            for r in range(q, PANELS):
+                upd = dot3((uth[BLK[p, q]], utl[BLK[p, q]]), split(rp[r, p]))
+                cw[block(q, r), :] = cw[block(q, r), :] - upd
+        for r in range(p):
+            rp[r, p] = jnp.zeros((T, T), F32)
+
+    products(0)
+    reduce1(0)
+    g6.wait_recv()
+    forward_a(1)
+    for c in g4 + g5 + [g6]:
+        c.wait_send()
+        left_early.append(id(c))
+    factor(0)
+    reduce2(0)
+    finish_a(1)
+    factor(1)
+    gather1(0)
+    products(1)
+    reduce1(1)
+    gather2(0)
+    factor(2)
+    factor(3)
+    reduce2(1)
+    gather1(1)
+    gather2(1)
+    for c in s3[0][3:] + s3[1][3:]:
+        c.wait_recv()
+
+    for s in range(2):
+        xs = []
+        slot = col * 2 + s
+        which = jnp.int32(0)
+        is_panel = jnp.int32(0)
+        for m in range(PANELS):
+            hit = owner_ref[m] == slot
+            which = jnp.where(hit, m, which)
+            is_panel = jnp.where(hit, 1, is_panel)
+        mask = jnp.full((T, T), is_panel, jnp.int32) == 1
+        for p in range(PANELS):
+            acc = jnp.concatenate([sfull[p, s, h] for h in range(H)], axis=1)
+            for q in range(p):
+                acc = acc - dot3((uth[BLK[q, p]], utl[BLK[q, p]]), xs[q])
+            got = dot3((wh_ref[p], wl_ref[p]), split(acc))
+            xs.append(split(got))
+            out_ref[p * T:(p + 1) * T, s * T:(s + 1) * T] = jnp.where(mask, rp[which, p], got)
+    good = checks[0]
+    for c in checks[1:]:
+        good = jnp.logical_and(good, c)
+    good_ref[0] = good.astype(jnp.int32)
+    for c in sends:
+        if id(c) not in left_early:
+            c.wait_send()
+
+
+def fast(child_blocks, home_child, col_tiles, tile_owner):
+    sem = 120
+    vm = pltpu.VMEM
+    vmem = pl.BlockSpec(memory_space=pltpu.VMEM)
+    smem = pl.BlockSpec(memory_space=pltpu.SMEM)
+    panels, packed, table = pl.pallas_call(
+        sort_kernel,
+        out_shape=(
+            jax.ShapeDtypeStruct((PANELS, OWN * ROWS, T), F32),
+            jax.ShapeDtypeStruct((H, OWN * ROWS, REST * HW), F32),
+            jax.ShapeDtypeStruct((8, 128), jnp.int32),
+        ),
+        in_specs=[smem, smem, smem, vmem],
+        out_specs=(vmem, vmem, vmem),
+        name="sort_tiles",
+    )(home_child, col_tiles, tile_owner, child_blocks)
+    return pl.pallas_call(
+        kernel,
+        out_shape=(
+            jax.ShapeDtypeStruct((PANELS * T, 2 * T), F32),
+            jax.ShapeDtypeStruct((1,), jnp.int32),
+        ),
+        in_specs=[smem, vmem, vmem, vmem],
+        out_specs=(vmem, smem),
+        scratch_shapes=[
+            vm((4, 2, H, OWN * ROWS, REST * HW), F32),
+            vm((4, 2, OWN * ROWS, T), F32),
+            vm((4, 2, 8, 128), jnp.int32),
+            pltpu.SMEM((4, 2, 8, 128), jnp.int32),
+            vm((REST + 1, 8 * 128, HW), BF),
+            vm((REST + 1, 8 * 128, HW), BF),
+            vm((T, 1024), BF),
+            vm((T, 1024), BF),
+            vm((1024, T), BF),
+            vm((1024, T), BF),
+            vm((H, 4, 4, T, HW), F32),
+            vm((H, 3, 4, 128, HW), F32),
+            vm((H, 3, 4, 128, HW), F32),
+            vm((H, 4, 128, HW), F32),
+            vm((H, 4, 128, HW), F32),
+            vm((H, 3, 128, HW), F32),
+            vm((H, 3, 128, HW), F32),
+            vm((4, 2, H, T, HW), F32),
+            vm((GROWS, T), F32),
+            vm((GHALF, T), F32),
+            vm((3, GC, T), F32),
+            vm((3, GC, T), F32),
+            vm((GC, T), F32),
+            vm((GC, T), F32),
+            vm((3, GS, T), F32),
+            vm((3, GS, T), F32),
+            vm((4, GS, T), F32),
+            vm((4, GS, T), F32),
+            vm((T, T), F32),
+            vm((PANELS, T, T), BF),
+            vm((PANELS, T, T), BF),
+            vm((GROWS, T), F32),
+            vm((len(BLOCKS), T, T), BF),
+            vm((len(BLOCKS), T, T), BF),
+            vm((PANELS, PANELS, T, T), F32),
+            pltpu.SemaphoreType.DMA((sem,)),
+            pltpu.SemaphoreType.DMA((sem,)),
+            pltpu.SemaphoreType.DMA((1,)),
+        ],
+        compiler_params=pltpu.CompilerParams(
+            collective_id=0, has_side_effects=True, vmem_limit_bytes=60 * 1024 * 1024
+        ),
+        cost_estimate=pl.CostEstimate(flops=10**10, bytes_accessed=10**7, transcendentals=0),
+        name="front",
+    )(tile_owner, panels, packed, table)
 
 
 def broadcast(x, axis, root):
@@ -24,11 +552,11 @@
     return jnp.sum(jnp.where(matches, tile_owner[None, None, :], 0), axis=2)
 
 
-def body(child_blocks, home_child, col_tiles, tile_owner):
+def general(child_blocks, home_child, col_tiles, tile_owner):
     highest = lax.Precision.HIGHEST
     col_count = lax.axis_size("col")
     local_cols = FRONT_COLS // col_count
-    held = local_cols // TILE_WIDTH
+    held = local_cols // T
     my_col = lax.axis_index("col")
     first_held = my_col * held
     position = storage_positions(home_child, col_tiles, tile_owner)
@@ -39,18 +567,18 @@
     mine = (local_tile[:, :, None] == jnp.arange(held, dtype=jnp.int32)[None, None, :]).astype(
         jnp.float32
     )
-    shaped = piece_blocks.reshape(count, CHILD_ROWS, CHILD_TILES, TILE_WIDTH)
+    shaped = piece_blocks.reshape(count, ROWS, CT, T)
     placed = jnp.einsum("nrjc,njk->nrkc", shaped, mine, precision=highest)
-    placed = placed.reshape(count * CHILD_ROWS, local_cols)
+    placed = placed.reshape(count * ROWS, local_cols)
     front = placed
-    identity = jnp.eye(TILE_WIDTH, dtype=jnp.float32)
+    identity = jnp.eye(T, dtype=jnp.float32)
     results = []
     for step in range(PANELS):
         stored_at = tile_owner[step]
         holder = stored_at // held
-        offset = (stored_at - holder * held) * TILE_WIDTH
+        offset = (stored_at - holder * held) * T
         is_holder = holder == my_col
-        panel = lax.dynamic_slice_in_dim(front, offset, TILE_WIDTH, 1)
+        panel = lax.dynamic_slice_in_dim(front, offset, T, 1)
         panel = jnp.where(is_holder, panel, 0.0)
         gram_part = jnp.dot(panel.T, panel, precision=highest, preferred_element_type=jnp.float32)
         gram = lax.psum(gram_part, "row")
@@ -68,6 +596,12 @@
     return stacked
 
 
+def body(child_blocks, home_child, col_tiles, tile_owner):
+    args = (child_blocks, home_child, col_tiles, tile_owner)
+    out, good = fast(*args)
+    return lax.cond(good[0] == 1, lambda *a: out, general, *args)
+
+
 def solution(mesh):
     return jax.shard_map(
         body,

time: 1410 us -> 134 us (0.10)
  waiting for transfers between devices: 949 us -> 0 us
  other arithmetic: 243 us -> 0 us
  Pallas kernels: 0 us -> 114 us
  matrix products: 91.5 us -> 0 us
  local copies, waits for them, and re-layouts: 61.7 us -> 4.57 us
  blocking collectives: 20.2 us -> 0 us
  between operations: 31.7 us -> 14.1 us
    psum x12 -> x0, waiting for transfers between devices: 817 us -> none  [the longest x4 360 us: broadcast(): return lax.psum(jnp.where(mine, x, jnp.zeros_like(x)), axis)]
    another operation x36 -> x0, other arithmetic: 217 us -> none  [the longest x27 138 us: body(): lower = jnp.linalg.cholesky(gram)]
    all_gather x1 -> x0, waiting for transfers between devices: 132 us -> none  [body(): piece_blocks = lax.all_gather(child_blocks, 'col', axis=0, tiled=True)]
    pallas_call x0 -> x2, Pallas kernels: none -> 114 us  [the longest x1 110 us: fast(): pl.pallas_call(kernel, out_shape=(jax.ShapeDtypeStruct((PANELS * T, 2 * T...]
    dot_general x12 -> x0, matrix products: 77.2 us -> none  [the longest x4 29.7 us: body(): jnp.dot(basis.T, front, precision=highest, preferred_element_type=jnp.flo...]
    reshape x2 -> x0, local copies, waits for them, and re-layouts: 35.8 us -> none  [the longest x1 30.4 us: body(): shaped = piece_blocks.reshape(count, CHILD_ROWS, CHILD_TILES, TILE_WIDTH)]
    all_gather x1 -> x0, blocking collectives: 20.2 us -> none  [body(): piece_slots = lax.all_gather(position, 'col', axis=0, tiled=True)]
    another operation x37 -> x0, local copies, waits for them, and re-layouts: 15.7 us -> none  [the longest x29 15.6 us: body(): basis = jax.scipy.linalg.solve_triangular(lower, panel.T, lower=True).T]
  transfers between devices with their start and end apart: 13 -> 0, of which waited for: 13 -> 0; matrix products, arithmetic and copies ran while one was open for 1% -> 0% of each run, Pallas kernels for 0% -> 0%
where the time goes in v1:
time: 134 us; the launch traced here: 133 us
  Pallas kernels  114 us (85%)
  between operations  14.1 us (11%)
  local copies, waits for them, and re-layouts  4.57 us (3%)
    pallas_call x1, Pallas kernels, fast(): pl.pallas_call(kernel, out_shape=(jax.ShapeDtypeStruct((PANELS * T, 2 * T...  110 us
    unnamed x8, local copies, waits for them, and re-layouts  4.57 us
    pallas_call x1, Pallas kernels, fast(): pl.pallas_call(sort_kernel, out_shape=(jax.ShapeDtypeStruct((PANELS, OWN...  4.27 us

profile of v1, /device:TPU:1, one launch (start us, length us, event | category | flops | bytes accessed | tf_op | source)
XLA Modules:
  0.0 133.3 jit_solution(16104010092252695825)
XLA Ops:
  6.5 1.5 %copy.56.tiles_ref = s32[256,12]{1,0:T(8,128)} copy(s32[256,12]{0,1:T(8,128)} %param.11) | data formatting | bytes 24576 | tf_op args[2]
  8.0 4.3 %sort_tiles.1 = (f32[4,128,256]{2,1,0:T(8,128)}, f32[2,128,1024]{2,1,0:T(8,128)}, s32[8,128]{1,0:T(8,128)}) custom-call(s32[2]{0:T(128)} %home_ref.1, s32[256,12]{1,0:T(8,128)} %copy.56.tiles_ref, s32[32]{0:T(128)} %owner_ref.3, f32[2,64,3072]{2,1,0:T(8,128)} %blocks_ref.1), custom_call_target="tpu_custom_call" | custom-call | tf_op jit(solution)/shard_map/sort_tiles/pallas_call | solution.py:474
  12.3 0.0 copy-start.9
  12.3 0.0 copy-start.10
  12.3 0.0 copy-start.11
  12.3 110.1 %front.1 = (f32[1024,512]{1,0:T(8,128)}, s32[1]{0:T(128)}) custom-call(s32[32]{0:T(128)} %owner_ref.3, f32[4,128,256]{2,1,0:T(8,128)} %get-tuple-element.28.pown, f32[2,128,1024]{2,1,0:T(8,128)} %get-tuple-element.29.packed_ref, s32[8,128]{1,0:T(8,128)} %get-tuple-element.30.table_ref), custom_call_target="tpu_custom_call" | custom-call | flops 10000000000 | bytes 10000000 | tf_op jit(solution)/shard_map/front/pallas_call | solution.py:485
  123.1 0.0 copy-done.9
  123.1 0.0 copy-done.10
  123.1 0.0 copy-done.11
  123.1 0.2 conditional.1
  123.4 3.1 %copy.123 = f32[1024,512]{1,0:T(8,128)} copy(f32[1024,512]{1,0:T(8,128)} %get-tuple-element.33) | data formatting | bytes 4194304
Async XLA Ops:
  12.3 110.8 %copy-start.9 = (s32[256,12]{0,1:T(8,128)S(1)}, s32[256,12]{0,1:T(8,128)}, u32[]{:S(2)}) copy-start(s32[256,12]{0,1:T(8,128)} %param.11) | copy-start | bytes 36868
  12.3 110.8 %copy-start.10 = (s32[32]{0:T(128)S(1)}, s32[32]{0:T(128)}, u32[]{:S(2)}) copy-start(s32[32]{0:T(128)} %owner_ref.3) | copy-start | bytes 388
  12.3 110.8 %copy-start.11 = (s32[2]{0:T(128)S(1)}, s32[2]{0:T(128)}, u32[]{:S(2)}) copy-start(s32[2]{0:T(128)} %home_ref.1) | copy-start | bytes 28

commit v2 on v1

--- a/solution.py
+++ b/solution.py
@@ -46,7 +46,55 @@
     return dg(ah, bh, ca, cb) + (dg(ah, bl, ca, cb) + dg(al, bh, ca, cb))
 
 
-def sort_kernel(home_ref, tiles_ref, owner_ref, blocks_ref, panels_ref, packed_ref, table_ref):
+def kernel(
+    home_ref, tiles_ref, owner_ref, blocks_ref,
+    out_ref, good_ref,
+    ag, pown, pg, tab, tab_s, agh, agl, pth, ptl, bh, bl, sp,
+    ra, rb, sa, sb, ra2, rb2, sfull,
+    gbuf, grc, ga, gb, gsa, gsb, ga2, gb2, gza, gzb,
+    wref, wh_ref, wl_ref, cw, uth, utl, rp,
+    xsem_s, xsem_r, lsem,
+):
+    row = lax.axis_index("row")
+    col = lax.axis_index("col")
+    z = row // 2
+    k = row % 2
+    y = col // 4
+    x = col % 4
+    sib = (z * 2 + (1 - k), col)
+
+    def zp(d):
+        return (lax.rem(z + d, 4) * 2 + k, col)
+
+    def xp(d):
+        return (row, y * 4 + lax.rem(x + d, 4))
+
+    def yp(d):
+        return (row, lax.rem(y + d, 4) * 4 + x)
+
+    barrier = pltpu.get_barrier_semaphore()
+    partners = [sib] + [f(d) for f in (zp, xp, yp) for d in (1, 2, 3)]
+    for dev in partners:
+        pl.semaphore_signal(barrier, inc=1, device_id=dev, device_id_type=MESH)
+
+    counter = [0]
+
+    def rcopy(src, dst, dev):
+        i = counter[0]
+        counter[0] += 1
+        return pltpu.make_async_remote_copy(
+            src_ref=src, dst_ref=dst, send_sem=xsem_s.at[i], recv_sem=xsem_r.at[i],
+            device_id=dev, device_id_type=MESH,
+        )
+
+    sends = []
+    left_early = []
+
+    def go(copy):
+        copy.start()
+        sends.append(copy)
+        return copy
+
     lane = lax.broadcasted_iota(jnp.int32, (8, 128), 1)
     sub = lax.broadcasted_iota(jnp.int32, (8, 128), 0)
     table = jnp.full((8, 128), REST, jnp.int32)
@@ -68,72 +116,20 @@
                 jnp.logical_and(jnp.logical_and(lane == p, sub == c), rest), count, table)
             count = count + rest.astype(jnp.int32)
         place.append((panel_at, rest_at))
-    table_ref[...] = table
+    tab[z, k] = table
     for c in range(OWN):
         for m in range(PANELS):
-            at = pl.multiple_of(place[c][0][m] * T, T)
-            panels_ref[m, c * ROWS:(c + 1) * ROWS, :] = blocks_ref[c, :, pl.ds(at, T)]
-        for i in range(REST):
-            at = pl.multiple_of(place[c][1][i] * T, T)
-            got = blocks_ref[c, :, pl.ds(at, T)]
-            for h in range(H):
-                packed_ref[h, c * ROWS:(c + 1) * ROWS, i * HW:(i + 1) * HW] = (
-                    got[:, h * HW:(h + 1) * HW])
-
-
-def kernel(
-    owner_ref, pown, packed_ref, table_ref,
-    out_ref, good_ref,
-    ag, pg, tab, tab_s, agh, agl, pth, ptl, bh, bl, sp,
-    ra, rb, sa, sb, ra2, rb2, sfull,
-    gbuf, grc, ga, gb, gsa, gsb, ga2, gb2, gza, gzb,
-    wref, wh_ref, wl_ref, cw, uth, utl, rp,
-    xsem_s, xsem_r, lsem,
-):
-    row = lax.axis_index("row")
-    col = lax.axis_index("col")
-    z = row // 2
-    k = row % 2
-    y = col // 4
-    x = col % 4
-    sib = (z * 2 + (1 - k), col)
-
-    def zp(d):
-        return (lax.rem(z + d, 4) * 2 + k, col)
-
-    def xp(d):
-        return (row, y * 4 + lax.rem(x + d, 4))
-
-    def yp(d):
-        return (row, lax.rem(y + d, 4) * 4 + x)
-
-    barrier = pltpu.get_barrier_semaphore()
-    partners = [sib] + [f(d) for f in (zp, xp, yp) for d in (1, 2, 3)]
-    for dev in partners:
-        pl.semaphore_signal(barrier, inc=1, device_id=dev, device_id_type=MESH)
-
-    counter = [0]
-
-    def rcopy(src, dst, dev):
-        i = counter[0]
-        counter[0] += 1
-        return pltpu.make_async_remote_copy(
-            src_ref=src, dst_ref=dst, send_sem=xsem_s.at[i], recv_sem=xsem_r.at[i],
-            device_id=dev, device_id_type=MESH,
-        )
-
-    sends = []
-    left_early = []
-
-    def go(copy):
-        copy.start()
-        sends.append(copy)
-        return copy
-
+            pown[m, c * ROWS:(c + 1) * ROWS, :] = blocks_ref[c, :, pl.ds(place[c][0][m] * T, T)]
+
+    def pack(h):
+        for c in range(OWN):
+            for i in range(REST):
+                at = place[c][1][i] * T + h * HW
+                ag[z, k, h, c * ROWS:(c + 1) * ROWS, i * HW:(i + 1) * HW] = (
+                    blocks_ref[c, :, pl.ds(at, HW)])
+
+    pack(0)
     pg[z, k] = pown[z]
-    tab[z, k] = table_ref[...]
-    for h in range(H):
-        ag[z, k, h] = packed_ref[h]
     pl.semaphore_wait(barrier, len(partners))
 
     pz, tz = [], []
@@ -202,6 +198,7 @@
     gk = pl.multiple_of(k * GHALF, GHALF)
     go_ = pl.multiple_of((1 - k) * GHALF, GHALF)
     g0 = go(rcopy(gbuf.at[pl.ds(go_, GHALF)], grc, sib))
+    pack(1)
     g0.wait_recv()
 
     def add_rows(dst, off, n, srcs):
@@ -239,6 +236,7 @@
         ox = pl.multiple_of(lax.rem(x + d, 4) * GS, GS)
         g2a.append(go(rcopy(gsa.at[pl.ds(oy, GS)], ga2.at[d - 1], yp(d))))
         g2b.append(go(rcopy(gsb.at[pl.ds(ox, GS)], gb2.at[d - 1], xp(d))))
+    forward_a(0)
     for c in g2a + g2b:
         c.wait_recv()
     oya = pl.multiple_of(y * GS, GS)
@@ -249,7 +247,7 @@
     for d in (1, 2, 3):
         g3.append(go(rcopy(gza.at[z], gza.at[z], zp(d))))
         g3.append(go(rcopy(gzb.at[z], gzb.at[z], zp(d))))
-    forward_a(0)
+    start_a(1)
     for c in g3:
         c.wait_recv()
     fa = pl.multiple_of(my_a + y * GS, GS)
@@ -264,6 +262,7 @@
         g4.append(go(rcopy(v, v, yp(d))))
         v = cw.at[pl.ds(fb, GS)]
         g4.append(go(rcopy(v, v, xp(d))))
+    finish_a(0)
     for c in g4:
         c.wait_recv()
     g5 = []
@@ -272,12 +271,6 @@
         g5.append(go(rcopy(v, v, xp(d))))
         v = cw.at[pl.ds(my_b, GC)]
         g5.append(go(rcopy(v, v, yp(d))))
-    finish_a(0)
-    for c in g5:
-        c.wait_recv()
-    v = cw.at[pl.ds(gk, GHALF)]
-    g6 = go(rcopy(v, v, sib))
-    start_a(1)
 
     for c in psib + tsib:
         c.wait_recv()
@@ -417,16 +410,42 @@
         for r in range(p):
             rp[r, p] = jnp.zeros((T, T), F32)
 
+    def solve(h):
+        xs = []
+        for p in range(PANELS):
+            acc = jnp.concatenate([sfull[p, s, h] for s in range(2)], axis=1)
+            for q in range(p):
+                acc = acc - dot3((uth[BLK[q, p]], utl[BLK[q, p]]), xs[q])
+            got = dot3((wh_ref[p], wl_ref[p]), split(acc))
+            if p < PANELS - 1:
+                xs.append(split(got))
+            for s in range(2):
+                slot = col * 2 + s
+                which = jnp.int32(0)
+                is_panel = jnp.int32(0)
+                for m in range(PANELS):
+                    hit = owner_ref[m] == slot
+                    which = jnp.where(hit, m, which)
+                    is_panel = jnp.where(hit, 1, is_panel)
+                mask = jnp.full((T, HW), is_panel, jnp.int32) == 1
+                at = s * T + h * HW
+                out_ref[p * T:(p + 1) * T, at:at + HW] = jnp.where(
+                    mask, rp[which, p, :, h * HW:(h + 1) * HW], got[:, s * HW:(s + 1) * HW])
+
     products(0)
     reduce1(0)
+    for c in g5:
+        c.wait_recv()
+    v = cw.at[pl.ds(gk, GHALF)]
+    g6 = go(rcopy(v, v, sib))
+    forward_a(1)
     g6.wait_recv()
-    forward_a(1)
     for c in g4 + g5 + [g6]:
         c.wait_send()
         left_early.append(id(c))
     factor(0)
+    finish_a(1)
     reduce2(0)
-    finish_a(1)
     factor(1)
     gather1(0)
     products(1)
@@ -434,29 +453,15 @@
     gather2(0)
     factor(2)
     factor(3)
+    for c in s3[0][3:]:
+        c.wait_recv()
     reduce2(1)
+    solve(0)
     gather1(1)
     gather2(1)
-    for c in s3[0][3:] + s3[1][3:]:
-        c.wait_recv()
-
-    for s in range(2):
-        xs = []
-        slot = col * 2 + s
-        which = jnp.int32(0)
-        is_panel = jnp.int32(0)
-        for m in range(PANELS):
-            hit = owner_ref[m] == slot
-            which = jnp.where(hit, m, which)
-            is_panel = jnp.where(hit, 1, is_panel)
-        mask = jnp.full((T, T), is_panel, jnp.int32) == 1
-        for p in range(PANELS):
-            acc = jnp.concatenate([sfull[p, s, h] for h in range(H)], axis=1)
-            for q in range(p):
-                acc = acc - dot3((uth[BLK[q, p]], utl[BLK[q, p]]), xs[q])
-            got = dot3((wh_ref[p], wl_ref[p]), split(acc))
-            xs.append(split(got))
-            out_ref[p * T:(p + 1) * T, s * T:(s + 1) * T] = jnp.where(mask, rp[which, p], got)
+    for c in s3[1][3:]:
+        c.wait_recv()
+    solve(1)
     good = checks[0]
     for c in checks[1:]:
         good = jnp.logical_and(good, c)
@@ -471,27 +476,17 @@
     vm = pltpu.VMEM
     vmem = pl.BlockSpec(memory_space=pltpu.VMEM)
     smem = pl.BlockSpec(memory_space=pltpu.SMEM)
-    panels, packed, table = pl.pallas_call(
-        sort_kernel,
-        out_shape=(
-            jax.ShapeDtypeStruct((PANELS, OWN * ROWS, T), F32),
-            jax.ShapeDtypeStruct((H, OWN * ROWS, REST * HW), F32),
-            jax.ShapeDtypeStruct((8, 128), jnp.int32),
-        ),
-        in_specs=[smem, smem, smem, vmem],
-        out_specs=(vmem, vmem, vmem),
-        name="sort_tiles",
-    )(home_child, col_tiles, tile_owner, child_blocks)
     return pl.pallas_call(
         kernel,
         out_shape=(
             jax.ShapeDtypeStruct((PANELS * T, 2 * T), F32),
             jax.ShapeDtypeStruct((1,), jnp.int32),
         ),
-        in_specs=[smem, vmem, vmem, vmem],
+        in_specs=[smem, smem, smem, vmem],
         out_specs=(vmem, smem),
         scratch_shapes=[
             vm((4, 2, H, OWN * ROWS, REST * HW), F32),
+            vm((PANELS, OWN * ROWS, T), F32),
             vm((4, 2, OWN * ROWS, T), F32),
             vm((4, 2, 8, 128), jnp.int32),
             pltpu.SMEM((4, 2, 8, 128), jnp.int32),
@@ -535,12 +530,33 @@
         ),
         cost_estimate=pl.CostEstimate(flops=10**10, bytes_accessed=10**7, transcendentals=0),
         name="front",
-    )(tile_owner, panels, packed, table)
+    )(home_child, col_tiles, tile_owner, child_blocks)
+
+
+def total(x, axis):
+    size = lax.axis_size(axis)
+    step = 1
+    while step < size:
+        x = x + lax.ppermute(x, axis, [(i, i ^ step) for i in range(size)])
+        step *= 2
+    return x
+
+
+def gathered(x, axis):
+    size = lax.axis_size(axis)
+    me = lax.axis_index(axis)
+    step = 1
+    while step < size:
+        other = lax.ppermute(x, axis, [(i, i ^ step) for i in range(size)])
+        low = (me // step) % 2 == 0
+        x = jnp.concatenate([jnp.where(low, x, other), jnp.where(low, other, x)], axis=0)
+        step *= 2
+    return x
 
 
 def broadcast(x, axis, root):
     mine = lax.axis_index(axis) == root
-    return lax.psum(jnp.where(mine, x, jnp.zeros_like(x)), axis)
+    return total(jnp.where(mine, x, jnp.zeros_like(x)), axis)
 
 
 def storage_positions(home_child, col_tiles, tile_owner):
@@ -560,8 +576,8 @@
     my_col = lax.axis_index("col")
     first_held = my_col * held
     position = storage_positions(home_child, col_tiles, tile_owner)
-    piece_blocks = lax.all_gather(child_blocks, "col", axis=0, tiled=True)
-    piece_slots = lax.all_gather(position, "col", axis=0, tiled=True)
+    piece_blocks = gathered(child_blocks, "col")
+    piece_slots = gathered(position, "col")
     count = piece_blocks.shape[0]
     local_tile = piece_slots - first_held
     mine = (local_tile[:, :, None] == jnp.arange(held, dtype=jnp.int32)[None, None, :]).astype(
@@ -581,13 +597,13 @@
         panel = lax.dynamic_slice_in_dim(front, offset, T, 1)
         panel = jnp.where(is_holder, panel, 0.0)
         gram_part = jnp.dot(panel.T, panel, precision=highest, preferred_element_type=jnp.float32)
-        gram = lax.psum(gram_part, "row")
+        gram = total(gram_part, "row")
         gram = gram + jnp.where(is_holder, 0.0, identity)
         lower = jnp.linalg.cholesky(gram)
         basis = jax.scipy.linalg.solve_triangular(lower, panel.T, lower=True).T
         basis = broadcast(basis, "col", holder)
         local_proj = jnp.dot(basis.T, front, precision=highest, preferred_element_type=jnp.float32)
-        projected = lax.psum(local_proj, "row")
+        projected = total(local_proj, "row")
         front = front - jnp.dot(
             basis, projected, precision=highest, preferred_element_type=jnp.float32
         )

time: 134 us -> 112 us (0.84)
  between operations: 14.1 us -> 0.68 us
  Pallas kernels: 114 us -> 107 us
    pallas_call x1 -> x0, Pallas kernels: 4.27 us -> none  [fast(): pl.pallas_call(sort_kernel, out_shape=(jax.ShapeDtypeStruct((PANELS, OWN...]
    pallas_call x1, Pallas kernels: 110 us -> 107 us  [fast(): pl.pallas_call(kernel, out_shape=(jax.ShapeDtypeStruct((PANELS * T, 2 * T...]
    unnamed x8 -> x10, local copies, waits for them, and re-layouts: 4.57 us -> 4.58 us
where the time goes in v2:
time: 112 us
  Pallas kernels  107 us (96%)
  local copies, waits for them, and re-layouts  4.58 us (4%)
    pallas_call x1, Pallas kernels, fast(): pl.pallas_call(kernel, out_shape=(jax.ShapeDtypeStruct((PANELS * T, 2 * T...  107 us
    unnamed x10, local copies, waits for them, and re-layouts  4.58 us

profile of v2, /device:TPU:1, one launch (start us, length us, event | category | flops | bytes accessed | tf_op | source)
XLA Modules:
  0.0 112.2 jit_solution(17353567010242528497)
XLA Ops:
  0.0 1.5 %copy.73.tiles_ref = s32[256,12]{1,0:T(8,128)} copy(s32[256,12]{0,1:T(8,128)} %param.11) | data formatting | bytes 24576 | tf_op args[2]
  1.5 0.0 copy-start.13
  1.5 0.0 copy-start.20
  1.5 0.0 copy-start.21
  1.5 0.0 copy-start.22
  1.5 106.7 %front.1 = (f32[1024,512]{1,0:T(8,128)}, s32[1]{0:T(128)}) custom-call(s32[2]{0:T(128)} %home_ref.1, s32[256,12]{1,0:T(8,128)} %copy.73.tiles_ref, s32[32]{0:T(128)} %owner_ref.1, f32[2,64,3072]{2,1,0:T(8,128)} %blocks_ref.1), custom_call_target="tpu_custom_call" | custom-call | flops 10000000000 | bytes 10000000 | tf_op jit(solution)/shard_map/front/pallas_call | solution.py:479
  108.8 0.0 copy-done.13
  108.8 0.0 copy-done.20
  108.9 0.0 copy-done.21
  108.9 0.0 copy-done.22
  108.9 0.2 conditional.1
  109.1 3.1 %copy.128 = f32[1024,512]{1,0:T(8,128)} copy(f32[1024,512]{1,0:T(8,128)} %get-tuple-element.27) | data formatting | bytes 4194304
Async XLA Ops:
  1.5 107.4 %copy-start.13 = (f32[2,64,3072]{2,1,0:T(8,128)S(1)}, f32[2,64,3072]{2,1,0:T(8,128)}, u32[]{:S(2)}) copy-start(f32[2,64,3072]{2,1,0:T(8,128)} %blocks_ref.1) | copy-start | bytes 4718596
  1.5 107.4 %copy-start.20 = (s32[256,12]{0,1:T(8,128)S(1)}, s32[256,12]{0,1:T(8,128)}, u32[]{:S(2)}) copy-start(s32[256,12]{0,1:T(8,128)} %param.11) | copy-start | bytes 36868
  1.5 107.4 %copy-start.21 = (s32[32]{0:T(128)S(1)}, s32[32]{0:T(128)}, u32[]{:S(2)}) copy-start(s32[32]{0:T(128)} %owner_ref.1) | copy-start | bytes 388
  1.5 107.4 %copy-start.22 = (s32[2]{0:T(128)S(1)}, s32[2]{0:T(128)}, u32[]{:S(2)}) copy-start(s32[2]{0:T(128)} %home_ref.1) | copy-start | bytes 28

commit v3 on v2

--- a/solution.py
+++ b/solution.py
@@ -15,8 +15,9 @@
 REST = CT - PANELS
 H = 2
 HW = T // H
-NEWTON = 4
-RESIDUAL = 1e-5
+NEWTON = 3
+SEM_FIX = 120
+RESIDUAL = 8e-5
 SHARE = 0.1
 F32 = jnp.float32
 BF = jnp.bfloat16
@@ -132,52 +133,58 @@
     pg[z, k] = pown[z]
     pl.semaphore_wait(barrier, len(partners))
 
+    def rows(c):
+        return pl.ds(c * ROWS, ROWS)
+
+    ar, al_, asib = {}, {}, {}
+
+    def start_sib(h):
+        mine = ag.at[z, k, h]
+        asib[h] = [go(rcopy(mine, mine, sib))]
+
+    def start_near(h, c):
+        me = ag.at[z, k, h, rows(c)]
+        ar[h, c] = go(rcopy(me, me, zp(1)))
+        other = ag.at[z, k, h, rows(1 - c)]
+        al_[h, 1 - c] = go(rcopy(other, other, zp(3)))
+
+    fr, fl = {}, {}
+    left = lax.rem(z + 3, 4)
+    right = lax.rem(z + 1, 4)
+    far = lax.rem(z + 2, 4)
+
+    def forward_a(h):
+        ar[h, 0].wait_recv()
+        v = ag.at[left, k, h, rows(0)]
+        fr[h] = go(rcopy(v, v, zp(1)))
+        al_[h, 1].wait_recv()
+        v = ag.at[right, k, h, rows(1)]
+        fl[h] = go(rcopy(v, v, zp(3)))
+
+    def sib_a(h):
+        ar[h, 1].wait_recv()
+        v = ag.at[left, k, h]
+        asib[h].append(go(rcopy(v, v, sib)))
+        al_[h, 0].wait_recv()
+        v = ag.at[right, k, h]
+        asib[h].append(go(rcopy(v, v, sib)))
+
+    def finish_a(h):
+        fr[h].wait_recv()
+        fl[h].wait_recv()
+        v = ag.at[far, k, h]
+        asib[h].append(go(rcopy(v, v, sib)))
+
+    start_near(0, 0)
+    start_near(0, 1)
+    start_sib(0)
+
     pz, tz = [], []
     for d in (1, 2, 3):
         pz.append(go(rcopy(pown.at[lax.rem(z + d, 4)], pg.at[z, k], zp(d))))
         tz.append(go(rcopy(tab.at[z, k], tab.at[z, k], zp(d))))
     psib = [go(rcopy(pown.at[z], pg.at[z, k], sib))]
     tsib = [go(rcopy(tab.at[z, k], tab.at[z, k], sib))]
-
-    def rows(c):
-        return pl.ds(c * ROWS, ROWS)
-
-    ar, al_, asib = {}, {}, {}
-
-    def start_a(h):
-        for c in range(OWN):
-            me = ag.at[z, k, h, rows(c)]
-            ar[h, c] = go(rcopy(me, me, zp(1)))
-            other = ag.at[z, k, h, rows(1 - c)]
-            al_[h, 1 - c] = go(rcopy(other, other, zp(3)))
-        mine = ag.at[z, k, h]
-        asib[h] = [go(rcopy(mine, mine, sib))]
-
-    start_a(0)
-    fr, fl = {}, {}
-
-    def forward_a(h):
-        left = lax.rem(z + 3, 4)
-        right = lax.rem(z + 1, 4)
-        ar[h, 0].wait_recv()
-        v = ag.at[left, k, h, rows(0)]
-        fr[h] = go(rcopy(v, v, zp(1)))
-        al_[h, 1].wait_recv()
-        v = ag.at[right, k, h, rows(1)]
-        fl[h] = go(rcopy(v, v, zp(3)))
-        ar[h, 1].wait_recv()
-        v = ag.at[left, k, h]
-        asib[h].append(go(rcopy(v, v, sib)))
-        al_[h, 0].wait_recv()
-        v = ag.at[right, k, h]
-        asib[h].append(go(rcopy(v, v, sib)))
-
-    def finish_a(h):
-        far = lax.rem(z + 2, 4)
-        fr[h].wait_recv()
-        fl[h].wait_recv()
-        v = ag.at[far, k, h]
-        asib[h].append(go(rcopy(v, v, sib)))
 
     def forward_p():
         for i, d in enumerate((1, 2, 3)):
@@ -223,7 +230,9 @@
         oy = pl.multiple_of(base_b + lax.rem(y + d, 4) * GC, GC)
         g1a.append(go(rcopy(gbuf.at[pl.ds(ox, GC)], ga.at[d - 1], xp(d))))
         g1b.append(go(rcopy(gbuf.at[pl.ds(oy, GC)], gb.at[d - 1], yp(d))))
-    forward_p()
+    start_sib(1)
+    forward_a(0)
+    start_near(1, 0)
     for c in g1a + g1b:
         c.wait_recv()
     my_a = pl.multiple_of(base_a + x * GC, GC)
@@ -236,7 +245,8 @@
         ox = pl.multiple_of(lax.rem(x + d, 4) * GS, GS)
         g2a.append(go(rcopy(gsa.at[pl.ds(oy, GS)], ga2.at[d - 1], yp(d))))
         g2b.append(go(rcopy(gsb.at[pl.ds(ox, GS)], gb2.at[d - 1], xp(d))))
-    forward_a(0)
+    sib_a(0)
+    forward_p()
     for c in g2a + g2b:
         c.wait_recv()
     oya = pl.multiple_of(y * GS, GS)
@@ -247,30 +257,8 @@
     for d in (1, 2, 3):
         g3.append(go(rcopy(gza.at[z], gza.at[z], zp(d))))
         g3.append(go(rcopy(gzb.at[z], gzb.at[z], zp(d))))
-    start_a(1)
-    for c in g3:
-        c.wait_recv()
-    fa = pl.multiple_of(my_a + y * GS, GS)
-    fb = pl.multiple_of(my_b + x * GS, GS)
-    gfin_a = gza[0] + gza[1] + gza[2] + gza[3]
-    gfin_b = gzb[0] + gzb[1] + gzb[2] + gzb[3]
-    cw[pl.ds(fa, GS), :] = gfin_a
-    cw[pl.ds(fb, GS), :] = gfin_b
-    g4 = []
-    for d in (1, 2, 3):
-        v = cw.at[pl.ds(fa, GS)]
-        g4.append(go(rcopy(v, v, yp(d))))
-        v = cw.at[pl.ds(fb, GS)]
-        g4.append(go(rcopy(v, v, xp(d))))
+    start_near(1, 1)
     finish_a(0)
-    for c in g4:
-        c.wait_recv()
-    g5 = []
-    for d in (1, 2, 3):
-        v = cw.at[pl.ds(my_a, GC)]
-        g5.append(go(rcopy(v, v, xp(d))))
-        v = cw.at[pl.ds(my_b, GC)]
-        g5.append(go(rcopy(v, v, yp(d))))
 
     for c in psib + tsib:
         c.wait_recv()
@@ -299,44 +287,99 @@
 
         lax.fori_loop(0, 8, conv, 0)
 
-        def pair(i, carry):
-            for s in range(2):
-                slot = (2 * i + s) * 2 + k
-                for n in range(16):
-                    at = tab_s[n // 4, (n // 2) % 2, n % 2, slot]
-                    bh[n * ROWS:(n + 1) * ROWS, s * HW:(s + 1) * HW] = (
-                        agh[at, n * ROWS:(n + 1) * ROWS, :])
-                    bl[n * ROWS:(n + 1) * ROWS, s * HW:(s + 1) * HW] = (
-                        agl[at, n * ROWS:(n + 1) * ROWS, :])
-            got = dot3((pth[...], ptl[...]), (bh[...], bl[...]))
-            yy = (2 * i) // 4
-            xx = lax.rem(2 * i, 4)
-            sp[h, yy, xx] = got[:, 0:HW]
-            sp[h, yy, xx + 1] = got[:, HW:]
-            return carry
-
-        lax.fori_loop(0, 8, pair, 0)
-
-    s1, s2, s3 = {}, {}, {}
-
-    def reduce1(h):
-        s1[h] = []
+        for part in range(2):
+            j = x // 2 if part else 1 - x // 2
+
+            def pair(a, carry, part=part, j=j):
+                yy = lax.rem(y + a, 4)
+                for s in range(2):
+                    slot = (yy * 4 + 2 * j + s) * 2 + k
+                    for n in range(16):
+                        at = tab_s[n // 4, (n // 2) % 2, n % 2, slot]
+                        bh[n * ROWS:(n + 1) * ROWS, s * HW:(s + 1) * HW] = (
+                            agh[at, n * ROWS:(n + 1) * ROWS, :])
+                        bl[n * ROWS:(n + 1) * ROWS, s * HW:(s + 1) * HW] = (
+                            agl[at, n * ROWS:(n + 1) * ROWS, :])
+                got = dot3((pth[...], ptl[...]), (bh[...], bl[...]))
+                sp[h, yy, 2 * j] = got[:, 0:HW]
+                sp[h, yy, 2 * j + 1] = got[:, HW:]
+                if part:
+                    first(h, 2 * j + 1 - lax.rem(x, 2), yy).start()
+                else:
+                    first(h, 2 * j, yy).start()
+                    first(h, 2 * j + 1, yy).start()
+
+                @pl.when(a < 4)
+                def _():
+                    second(h, yy, j).start()
+
+                return carry
+
+            lax.fori_loop(1, 5, pair, 0)
+
+    base1 = SEM_FIX
+
+    def first(h, px, yy):
+        at = base1 + h * 24
+        return pltpu.make_async_remote_copy(
+            src_ref=sp.at[h, yy, px, pl.ds(0, 128)], dst_ref=ra.at[h, x, yy],
+            send_sem=xsem_s.at[at + 4 * px + yy], recv_sem=xsem_r.at[at + 4 * x + yy],
+            device_id=(row, y * 4 + px), device_id_type=MESH,
+        )
+
+    def first_in(h, px, yy):
+        at = base1 + h * 24
+        return pltpu.make_async_remote_copy(
+            src_ref=sp.at[h, yy, px, pl.ds(0, 128)], dst_ref=ra.at[h, px, yy],
+            send_sem=xsem_s.at[at + 4 * px + yy], recv_sem=xsem_r.at[at + 4 * px + yy],
+            device_id=(row, y * 4 + px), device_id_type=MESH,
+        )
+
+    def second(h, py, j):
+        at = base1 + h * 24 + 16
+        return pltpu.make_async_remote_copy(
+            src_ref=sp.at[h, py, pl.ds(2 * j, 2), pl.ds(128, 128)],
+            dst_ref=rb.at[h, y, pl.ds(2 * j, 2)],
+            send_sem=xsem_s.at[at + 2 * py + j], recv_sem=xsem_r.at[at + 2 * y + j],
+            device_id=(row, py * 4 + x), device_id_type=MESH,
+        )
+
+    def second_in(h, py, j):
+        at = base1 + h * 24 + 16
+        return pltpu.make_async_remote_copy(
+            src_ref=sp.at[h, py, pl.ds(2 * j, 2), pl.ds(128, 128)],
+            dst_ref=rb.at[h, py, pl.ds(2 * j, 2)],
+            send_sem=xsem_s.at[at + 2 * py + j], recv_sem=xsem_r.at[at + 2 * py + j],
+            device_id=(row, py * 4 + x), device_id_type=MESH,
+        )
+
+    s2, s3 = {}, {}
+
+    def reduce2(h):
         for d in (1, 2, 3):
-            s1[h].append(go(rcopy(
-                sp.at[h, :, lax.rem(x + d, 4), pl.ds(0, 128)], ra.at[h, d - 1], xp(d))))
-            s1[h].append(go(rcopy(
-                sp.at[h, lax.rem(y + d, 4), :, pl.ds(128, 128)], rb.at[h, d - 1], yp(d))))
-
-    def reduce2(h):
-        for c in s1[h]:
-            c.wait_recv()
+            for i in range(4):
+                first_in(h, lax.rem(x + d, 4), i).wait_recv()
+            for j in range(2):
+                second_in(h, lax.rem(y + d, 4), j).wait_recv()
         for i in range(4):
-            sa[h, i] = sp[h, i, x, 0:128, :] + ra[h, 0, i] + ra[h, 1, i] + ra[h, 2, i]
-            sb[h, i] = sp[h, y, i, 128:256, :] + rb[h, 0, i] + rb[h, 1, i] + rb[h, 2, i]
+            va = sp[h, i, x, 0:128, :]
+            vb = sp[h, y, i, 128:256, :]
+            for d in (1, 2, 3):
+                va = va + ra[h, lax.rem(x + d, 4), i]
+                vb = vb + rb[h, lax.rem(y + d, 4), i]
+            sa[h, i] = va
+            sb[h, i] = vb
         s2[h] = []
         for d in (1, 2, 3):
             s2[h].append(go(rcopy(sa.at[h, lax.rem(y + d, 4)], ra2.at[h, d - 1], yp(d))))
             s2[h].append(go(rcopy(sb.at[h, lax.rem(x + d, 4)], rb2.at[h, d - 1], xp(d))))
+
+    def sent1(h):
+        for d in (1, 2, 3):
+            for i in range(4):
+                first_in(h, lax.rem(x + d, 4), i).wait_send()
+            for j in range(2):
+                second_in(h, lax.rem(y + d, 4), j).wait_send()
 
     def gather1(h):
         for c in s2[h]:
@@ -433,31 +476,52 @@
                     mask, rp[which, p, :, h * HW:(h + 1) * HW], got[:, s * HW:(s + 1) * HW])
 
     products(0)
-    reduce1(0)
+    forward_a(1)
+    for c in g3:
+        c.wait_recv()
+    fa = pl.multiple_of(my_a + y * GS, GS)
+    fb = pl.multiple_of(my_b + x * GS, GS)
+    gfin_a = gza[0] + gza[1] + gza[2] + gza[3]
+    gfin_b = gzb[0] + gzb[1] + gzb[2] + gzb[3]
+    cw[pl.ds(fa, GS), :] = gfin_a
+    cw[pl.ds(fb, GS), :] = gfin_b
+    g4 = []
+    for d in (1, 2, 3):
+        v = cw.at[pl.ds(fa, GS)]
+        g4.append(go(rcopy(v, v, yp(d))))
+        v = cw.at[pl.ds(fb, GS)]
+        g4.append(go(rcopy(v, v, xp(d))))
+    sib_a(1)
+    reduce2(0)
+    finish_a(1)
+    for c in g4:
+        c.wait_recv()
+    g5 = []
+    for d in (1, 2, 3):
+        v = cw.at[pl.ds(my_a, GC)]
+        g5.append(go(rcopy(v, v, xp(d))))
+        v = cw.at[pl.ds(my_b, GC)]
+        g5.append(go(rcopy(v, v, yp(d))))
+    products(1)
+    gather1(0)
     for c in g5:
         c.wait_recv()
     v = cw.at[pl.ds(gk, GHALF)]
     g6 = go(rcopy(v, v, sib))
-    forward_a(1)
+    gather2(0)
     g6.wait_recv()
     for c in g4 + g5 + [g6]:
         c.wait_send()
         left_early.append(id(c))
     factor(0)
-    finish_a(1)
-    reduce2(0)
     factor(1)
-    gather1(0)
-    products(1)
-    reduce1(1)
-    gather2(0)
+    reduce2(1)
     factor(2)
+    gather1(1)
     factor(3)
     for c in s3[0][3:]:
         c.wait_recv()
-    reduce2(1)
     solve(0)
-    gather1(1)
     gather2(1)
     for c in s3[1][3:]:
         c.wait_recv()
@@ -469,10 +533,12 @@
     for c in sends:
         if id(c) not in left_early:
             c.wait_send()
+    for h in range(H):
+        sent1(h)
 
 
 def fast(child_blocks, home_child, col_tiles, tile_owner):
-    sem = 120
+    sem = SEM_FIX + 48
     vm = pltpu.VMEM
     vmem = pl.BlockSpec(memory_space=pltpu.VMEM)
     smem = pl.BlockSpec(memory_space=pltpu.SMEM)
@@ -497,8 +563,8 @@
             vm((1024, T), BF),
             vm((1024, T), BF),
             vm((H, 4, 4, T, HW), F32),
-            vm((H, 3, 4, 128, HW), F32),
-            vm((H, 3, 4, 128, HW), F32),
+            vm((H, 4, 4, 128, HW), F32),
+            vm((H, 4, 4, 128, HW), F32),
             vm((H, 4, 128, HW), F32),
             vm((H, 4, 128, HW), F32),
             vm((H, 3, 128, HW), F32),

time: 112 us -> 106 us (0.946)
  Pallas kernels: 107 us -> 99.7 us
    pallas_call x1, Pallas kernels: 107 us -> 99.7 us  [fast(): pl.pallas_call(kernel, out_shape=(jax.ShapeDtypeStruct((PANELS * T, 2 * T...]
where the time goes in v3:
time: 106 us; the launch traced here: 105 us
  Pallas kernels  99.7 us (94%)
  local copies, waits for them, and re-layouts  4.58 us (4%)
    pallas_call x1, Pallas kernels, fast(): pl.pallas_call(kernel, out_shape=(jax.ShapeDtypeStruct((PANELS * T, 2 * T...  99.7 us
    unnamed x10, local copies, waits for them, and re-layouts  4.58 us

profile of v3, /device:TPU:1, one launch (start us, length us, event | category | flops | bytes accessed | tf_op | source)
XLA Modules:
  0.0 105.2 jit_solution(1675451518806904231)
XLA Ops:
  0.0 1.5 %copy.73.tiles_ref = s32[256,12]{1,0:T(8,128)} copy(s32[256,12]{0,1:T(8,128)} %param.11) | data formatting | bytes 24576 | tf_op args[2]
  1.5 0.0 copy-start.13
  1.5 0.0 copy-start.20
  1.5 0.0 copy-start.21
  1.5 0.0 copy-start.22
  1.5 99.7 %front.1 = (f32[1024,512]{1,0:T(8,128)}, s32[1]{0:T(128)}) custom-call(s32[2]{0:T(128)} %home_ref.1, s32[256,12]{1,0:T(8,128)} %copy.73.tiles_ref, s32[32]{0:T(128)} %owner_ref.1, f32[2,64,3072]{2,1,0:T(8,128)} %blocks_ref.1), custom_call_target="tpu_custom_call" | custom-call | flops 10000000000 | bytes 10000000 | tf_op jit(solution)/shard_map/front/pallas_call | solution.py:545
  101.8 0.0 copy-done.13
  101.8 0.0 copy-done.20
  101.9 0.0 copy-done.21
  101.9 0.0 copy-done.22
  101.9 0.3 conditional.1
  102.2 3.1 %copy.128 = f32[1024,512]{1,0:T(8,128)} copy(f32[1024,512]{1,0:T(8,128)} %get-tuple-element.27) | data formatting | bytes 4194304
Async XLA Ops:
  1.5 100.4 %copy-start.13 = (f32[2,64,3072]{2,1,0:T(8,128)S(1)}, f32[2,64,3072]{2,1,0:T(8,128)}, u32[]{:S(2)}) copy-start(f32[2,64,3072]{2,1,0:T(8,128)} %blocks_ref.1) | copy-start | bytes 4718596
  1.5 100.4 %copy-start.20 = (s32[256,12]{0,1:T(8,128)S(1)}, s32[256,12]{0,1:T(8,128)}, u32[]{:S(2)}) copy-start(s32[256,12]{0,1:T(8,128)} %param.11) | copy-start | bytes 36868
  1.5 100.4 %copy-start.21 = (s32[32]{0:T(128)S(1)}, s32[32]{0:T(128)}, u32[]{:S(2)}) copy-start(s32[32]{0:T(128)} %owner_ref.1) | copy-start | bytes 388
  1.5 100.4 %copy-start.22 = (s32[2]{0:T(128)S(1)}, s32[2]{0:T(128)}, u32[]{:S(2)}) copy-start(s32[2]{0:T(128)} %home_ref.1) | copy-start | bytes 28

commit v4 on v3

--- a/solution.py
+++ b/solution.py
@@ -13,10 +13,11 @@
 PANELS = 4
 OWN = 2
 REST = CT - PANELS
-H = 2
-HW = T // H
+H = 4
+QW = T // H
+HW = 2 * QW
 NEWTON = 3
-SEM_FIX = 120
+SEM_FIX = 140
 RESIDUAL = 8e-5
 SHARE = 0.1
 F32 = jnp.float32
@@ -122,14 +123,24 @@
         for m in range(PANELS):
             pown[m, c * ROWS:(c + 1) * ROWS, :] = blocks_ref[c, :, pl.ds(place[c][0][m] * T, T)]
 
+    def low(shape):
+        return lax.broadcasted_iota(jnp.int32, shape, 1) < QW
+
+    def swap(v):
+        return pltpu.roll(v, QW, 1)
+
     def pack(h):
         for c in range(OWN):
-            for i in range(REST):
-                at = place[c][1][i] * T + h * HW
-                ag[z, k, h, c * ROWS:(c + 1) * ROWS, i * HW:(i + 1) * HW] = (
-                    blocks_ref[c, :, pl.ds(at, HW)])
+            for i in range(0, REST, 2):
+                a, b = (
+                    blocks_ref[c, :, pl.ds(place[c][1][i + n] * T + h // 2 * HW, HW)]
+                    for n in range(2))
+                both = (swap(a), b) if h % 2 else (a, swap(b))
+                ag[z, k, h, c * ROWS:(c + 1) * ROWS, i * QW:(i + 2) * QW] = jnp.where(
+                    low((ROWS, HW)), *both)
 
     pack(0)
+    pack(1)
     pg[z, k] = pown[z]
     pl.semaphore_wait(barrier, len(partners))
 
@@ -175,16 +186,14 @@
         v = ag.at[far, k, h]
         asib[h].append(go(rcopy(v, v, sib)))
 
-    start_near(0, 0)
-    start_near(0, 1)
-    start_sib(0)
-
-    pz, tz = [], []
-    for d in (1, 2, 3):
-        pz.append(go(rcopy(pown.at[lax.rem(z + d, 4)], pg.at[z, k], zp(d))))
-        tz.append(go(rcopy(tab.at[z, k], tab.at[z, k], zp(d))))
-    psib = [go(rcopy(pown.at[z], pg.at[z, k], sib))]
-    tsib = [go(rcopy(tab.at[z, k], tab.at[z, k], sib))]
+    pz, tz, psib, tsib = [], [], [], []
+
+    def start_p():
+        for d in (1, 2, 3):
+            pz.append(go(rcopy(pown.at[lax.rem(z + d, 4)], pg.at[z, k], zp(d))))
+            tz.append(go(rcopy(tab.at[z, k], tab.at[z, k], zp(d))))
+        psib.append(go(rcopy(pown.at[z], pg.at[z, k], sib)))
+        tsib.append(go(rcopy(tab.at[z, k], tab.at[z, k], sib)))
 
     def forward_p():
         for i, d in enumerate((1, 2, 3)):
@@ -201,12 +210,8 @@
         for i, (q, r) in enumerate(BLOCKS):
             gbuf[i * T:(i + 1) * T, :] = dot3(halves[q], halves[r], 0, 0)
 
-    gram()
     gk = pl.multiple_of(k * GHALF, GHALF)
     go_ = pl.multiple_of((1 - k) * GHALF, GHALF)
-    g0 = go(rcopy(gbuf.at[pl.ds(go_, GHALF)], grc, sib))
-    pack(1)
-    g0.wait_recv()
 
     def add_rows(dst, off, n, srcs):
         step = 160 if n % 160 == 0 else n
@@ -221,57 +226,93 @@
 
         lax.fori_loop(0, n // step, body, 0)
 
-    add_rows(gbuf, gk, GHALF, [grc])
-    base_a = gk
     base_b = pl.multiple_of(gk + GQ, GQ)
-    g1a, g1b = [], []
-    for d in (1, 2, 3):
-        ox = pl.multiple_of(base_a + lax.rem(x + d, 4) * GC, GC)
-        oy = pl.multiple_of(base_b + lax.rem(y + d, 4) * GC, GC)
-        g1a.append(go(rcopy(gbuf.at[pl.ds(ox, GC)], ga.at[d - 1], xp(d))))
-        g1b.append(go(rcopy(gbuf.at[pl.ds(oy, GC)], gb.at[d - 1], yp(d))))
-    start_sib(1)
-    forward_a(0)
-    start_near(1, 0)
-    for c in g1a + g1b:
-        c.wait_recv()
-    my_a = pl.multiple_of(base_a + x * GC, GC)
+    my_a = pl.multiple_of(gk + x * GC, GC)
     my_b = pl.multiple_of(base_b + y * GC, GC)
-    gsa[...] = gbuf[pl.ds(my_a, GC), :] + ga[0] + ga[1] + ga[2]
-    gsb[...] = gbuf[pl.ds(my_b, GC), :] + gb[0] + gb[1] + gb[2]
-    g2a, g2b = [], []
-    for d in (1, 2, 3):
-        oy = pl.multiple_of(lax.rem(y + d, 4) * GS, GS)
-        ox = pl.multiple_of(lax.rem(x + d, 4) * GS, GS)
-        g2a.append(go(rcopy(gsa.at[pl.ds(oy, GS)], ga2.at[d - 1], yp(d))))
-        g2b.append(go(rcopy(gsb.at[pl.ds(ox, GS)], gb2.at[d - 1], xp(d))))
-    sib_a(0)
-    forward_p()
-    for c in g2a + g2b:
-        c.wait_recv()
-    oya = pl.multiple_of(y * GS, GS)
-    oxb = pl.multiple_of(x * GS, GS)
-    gza[z] = gsa[pl.ds(oya, GS), :] + ga2[0] + ga2[1] + ga2[2]
-    gzb[z] = gsb[pl.ds(oxb, GS), :] + gb2[0] + gb2[1] + gb2[2]
-    g3 = []
-    for d in (1, 2, 3):
-        g3.append(go(rcopy(gza.at[z], gza.at[z], zp(d))))
-        g3.append(go(rcopy(gzb.at[z], gzb.at[z], zp(d))))
-    start_near(1, 1)
-    finish_a(0)
-
-    for c in psib + tsib:
-        c.wait_recv()
-    tcopy = pltpu.make_async_copy(tab, tab_s, lsem.at[0])
-    tcopy.start()
-    for i in range(8):
-        hi, lo = split(jnp.transpose(pg[i // 2, i % 2]))
-        pth[:, i * 128:(i + 1) * 128] = hi
-        ptl[:, i * 128:(i + 1) * 128] = lo
-    tcopy.wait()
-    zero = jnp.zeros((8 * 128, HW), BF)
-    agh[REST] = zero
-    agl[REST] = zero
+    fa = pl.multiple_of(my_a + y * GS, GS)
+    fb = pl.multiple_of(my_b + x * GS, GS)
+    g = {n: [] for n in range(7)}
+
+    def sum0():
+        g[0].append(go(rcopy(gbuf.at[pl.ds(go_, GHALF)], grc, sib)))
+
+    def sum1():
+        g[0][0].wait_recv()
+        add_rows(gbuf, gk, GHALF, [grc])
+        for d in (1, 2, 3):
+            ox = pl.multiple_of(gk + lax.rem(x + d, 4) * GC, GC)
+            oy = pl.multiple_of(base_b + lax.rem(y + d, 4) * GC, GC)
+            g[1].append(go(rcopy(gbuf.at[pl.ds(ox, GC)], ga.at[d - 1], xp(d))))
+            g[1].append(go(rcopy(gbuf.at[pl.ds(oy, GC)], gb.at[d - 1], yp(d))))
+
+    def sum2():
+        for c in g[1]:
+            c.wait_recv()
+        gsa[...] = gbuf[pl.ds(my_a, GC), :] + ga[0] + ga[1] + ga[2]
+        gsb[...] = gbuf[pl.ds(my_b, GC), :] + gb[0] + gb[1] + gb[2]
+        for d in (1, 2, 3):
+            oy = pl.multiple_of(lax.rem(y + d, 4) * GS, GS)
+            ox = pl.multiple_of(lax.rem(x + d, 4) * GS, GS)
+            g[2].append(go(rcopy(gsa.at[pl.ds(oy, GS)], ga2.at[d - 1], yp(d))))
+            g[2].append(go(rcopy(gsb.at[pl.ds(ox, GS)], gb2.at[d - 1], xp(d))))
+
+    def sum3():
+        for c in g[2]:
+            c.wait_recv()
+        oya = pl.multiple_of(y * GS, GS)
+        oxb = pl.multiple_of(x * GS, GS)
+        gza[z] = gsa[pl.ds(oya, GS), :] + ga2[0] + ga2[1] + ga2[2]
+        gzb[z] = gsb[pl.ds(oxb, GS), :] + gb2[0] + gb2[1] + gb2[2]
+        for d in (1, 2, 3):
+            g[3].append(go(rcopy(gza.at[z], gza.at[z], zp(d))))
+            g[3].append(go(rcopy(gzb.at[z], gzb.at[z], zp(d))))
+
+    def back4():
+        for c in g[3]:
+            c.wait_recv()
+        cw[pl.ds(fa, GS), :] = gza[0] + gza[1] + gza[2] + gza[3]
+        cw[pl.ds(fb, GS), :] = gzb[0] + gzb[1] + gzb[2] + gzb[3]
+        for d in (1, 2, 3):
+            v = cw.at[pl.ds(fa, GS)]
+            g[4].append(go(rcopy(v, v, yp(d))))
+            v = cw.at[pl.ds(fb, GS)]
+            g[4].append(go(rcopy(v, v, xp(d))))
+
+    def back5():
+        for c in g[4]:
+            c.wait_recv()
+        for d in (1, 2, 3):
+            v = cw.at[pl.ds(my_a, GC)]
+            g[5].append(go(rcopy(v, v, xp(d))))
+            v = cw.at[pl.ds(my_b, GC)]
+            g[5].append(go(rcopy(v, v, yp(d))))
+
+    def back6():
+        for c in g[5]:
+            c.wait_recv()
+        v = cw.at[pl.ds(gk, GHALF)]
+        g[6].append(go(rcopy(v, v, sib)))
+
+    def gram_back():
+        g[6][0].wait_recv()
+        for c in g[4] + g[5] + g[6]:
+            c.wait_send()
+            left_early.append(id(c))
+
+    def ready_p():
+        for c in psib + tsib:
+            c.wait_recv()
+        tcopy = pltpu.make_async_copy(tab, tab_s, lsem.at[0])
+        tcopy.start()
+        for i in range(8):
+            hi, lo = split(jnp.transpose(pg[i // 2, i % 2]))
+            pth[:, i * 128:(i + 1) * 128] = hi
+            ptl[:, i * 128:(i + 1) * 128] = lo
+        tcopy.wait()
+        zero = jnp.zeros((8 * 128, HW), BF)
+        for i in range(2):
+            agh[REST + i] = zero
+            agl[REST + i] = zero
 
     def products(h):
         for c in asib[h]:
@@ -279,10 +320,12 @@
 
         def conv(i, carry):
             o = pl.multiple_of(i * 128, 128)
-            hi, lo = split(ag[i // 2, lax.rem(i, 2), h])
-            for t in range(REST):
-                agh[t, pl.ds(o, 128), :] = hi[:, t * HW:(t + 1) * HW]
-                agl[t, pl.ds(o, 128), :] = lo[:, t * HW:(t + 1) * HW]
+            for t in range(0, REST, 2):
+                v = ag[i // 2, lax.rem(i, 2), h, :, t * QW:(t + 2) * QW]
+                for n, w in enumerate((v, swap(v))):
+                    hi, lo = split(w)
+                    agh[t + n, pl.ds(o, 128), :] = hi
+                    agl[t + n, pl.ds(o, 128), :] = lo
             return carry
 
         lax.fori_loop(0, 8, conv, 0)
@@ -290,39 +333,50 @@
         for part in range(2):
             j = x // 2 if part else 1 - x // 2
 
-            def pair(a, carry, part=part, j=j):
-                yy = lax.rem(y + a, 4)
-                for s in range(2):
-                    slot = (yy * 4 + 2 * j + s) * 2 + k
+            def pair(b, carry, part=part, j=j):
+                mask = low((ROWS, HW))
+                rows_at = [lax.rem(y + 1 + 2 * b + u, 4) for u in range(2)]
+                for u in range(2):
+                    slot = (rows_at[u] * 4 + 2 * j) * 2 + k
                     for n in range(16):
-                        at = tab_s[n // 4, (n // 2) % 2, n % 2, slot]
-                        bh[n * ROWS:(n + 1) * ROWS, s * HW:(s + 1) * HW] = (
-                            agh[at, n * ROWS:(n + 1) * ROWS, :])
-                        bl[n * ROWS:(n + 1) * ROWS, s * HW:(s + 1) * HW] = (
-                            agl[at, n * ROWS:(n + 1) * ROWS, :])
+                        at0 = tab_s[n // 4, (n // 2) % 2, n % 2, slot]
+                        at1 = tab_s[n // 4, (n // 2) % 2, n % 2, slot + 2]
+                        at1 = at1 + 1 - 2 * lax.rem(at1, 2)
+                        rn = slice(n * ROWS, (n + 1) * ROWS)
+                        cn = slice(u * HW, (u + 1) * HW)
+                        bh[rn, cn] = jnp.where(mask, agh[at0, rn, :], agh[at1, rn, :])
+                        bl[rn, cn] = jnp.where(mask, agl[at0, rn, :], agl[at1, rn, :])
                 got = dot3((pth[...], ptl[...]), (bh[...], bl[...]))
-                sp[h, yy, 2 * j] = got[:, 0:HW]
-                sp[h, yy, 2 * j + 1] = got[:, HW:]
-                if part:
-                    first(h, 2 * j + 1 - lax.rem(x, 2), yy).start()
-                else:
-                    first(h, 2 * j, yy).start()
-                    first(h, 2 * j + 1, yy).start()
-
-                @pl.when(a < 4)
+                half = low((128, HW))
+                for u in range(2):
+                    top = got[0:128, u * HW:(u + 1) * HW]
+                    bottom = got[128:256, u * HW:(u + 1) * HW]
+                    yy = rows_at[u]
+                    sp[h, yy, 2 * j] = jnp.where(half, top, swap(bottom))
+                    sp[h, yy, 2 * j + 1] = jnp.where(half, swap(top), bottom)
+                for u in range(2):
+                    yy = rows_at[u]
+                    if part:
+                        first(h, 2 * j + 1 - lax.rem(x, 2), yy).start()
+                    else:
+                        first(h, 2 * j, yy).start()
+                        first(h, 2 * j + 1, yy).start()
+                second(h, rows_at[0], j).start()
+
+                @pl.when(b == 0)
                 def _():
-                    second(h, yy, j).start()
+                    second(h, rows_at[1], j).start()
 
                 return carry
 
-            lax.fori_loop(1, 5, pair, 0)
+            lax.fori_loop(0, 2, pair, 0)
 
     base1 = SEM_FIX
 
     def first(h, px, yy):
         at = base1 + h * 24
         return pltpu.make_async_remote_copy(
-            src_ref=sp.at[h, yy, px, pl.ds(0, 128)], dst_ref=ra.at[h, x, yy],
+            src_ref=sp.at[h, yy, px, pl.ds(0, 64)], dst_ref=ra.at[h, x, yy],
             send_sem=xsem_s.at[at + 4 * px + yy], recv_sem=xsem_r.at[at + 4 * x + yy],
             device_id=(row, y * 4 + px), device_id_type=MESH,
         )
@@ -330,7 +384,7 @@
     def first_in(h, px, yy):
         at = base1 + h * 24
         return pltpu.make_async_remote_copy(
-            src_ref=sp.at[h, yy, px, pl.ds(0, 128)], dst_ref=ra.at[h, px, yy],
+            src_ref=sp.at[h, yy, px, pl.ds(0, 64)], dst_ref=ra.at[h, px, yy],
             send_sem=xsem_s.at[at + 4 * px + yy], recv_sem=xsem_r.at[at + 4 * px + yy],
             device_id=(row, y * 4 + px), device_id_type=MESH,
         )
@@ -338,7 +392,7 @@
     def second(h, py, j):
         at = base1 + h * 24 + 16
         return pltpu.make_async_remote_copy(
-            src_ref=sp.at[h, py, pl.ds(2 * j, 2), pl.ds(128, 128)],
+            src_ref=sp.at[h, py, pl.ds(2 * j, 2), pl.ds(64, 64)],
             dst_ref=rb.at[h, y, pl.ds(2 * j, 2)],
             send_sem=xsem_s.at[at + 2 * py + j], recv_sem=xsem_r.at[at + 2 * y + j],
             device_id=(row, py * 4 + x), device_id_type=MESH,
@@ -347,7 +401,7 @@
     def second_in(h, py, j):
         at = base1 + h * 24 + 16
         return pltpu.make_async_remote_copy(
-            src_ref=sp.at[h, py, pl.ds(2 * j, 2), pl.ds(128, 128)],
+            src_ref=sp.at[h, py, pl.ds(2 * j, 2), pl.ds(64, 64)],
             dst_ref=rb.at[h, py, pl.ds(2 * j, 2)],
             send_sem=xsem_s.at[at + 2 * py + j], recv_sem=xsem_r.at[at + 2 * py + j],
             device_id=(row, py * 4 + x), device_id_type=MESH,
@@ -362,8 +416,8 @@
             for j in range(2):
                 second_in(h, lax.rem(y + d, 4), j).wait_recv()
         for i in range(4):
-            va = sp[h, i, x, 0:128, :]
-            vb = sp[h, y, i, 128:256, :]
+            va = sp[h, i, x, 0:64, :]
+            vb = sp[h, y, i, 64:128, :]
             for d in (1, 2, 3):
                 va = va + ra[h, lax.rem(x + d, 4), i]
                 vb = vb + rb[h, lax.rem(y + d, 4), i]
@@ -384,8 +438,8 @@
     def gather1(h):
         for c in s2[h]:
             c.wait_recv()
-        sfull[z, k, h, 0:128, :] = sa[h, y] + ra2[h, 0] + ra2[h, 1] + ra2[h, 2]
-        sfull[z, k, h, 128:256, :] = sb[h, x] + rb2[h, 0] + rb2[h, 1] + rb2[h, 2]
+        sfull[z, k, h, 0:64, :] = sa[h, y] + ra2[h, 0] + ra2[h, 1] + ra2[h, 2]
+        sfull[z, k, h, 64:128, :] = sb[h, x] + rb2[h, 0] + rb2[h, 1] + rb2[h, 2]
         v = sfull.at[z, k, h]
         s3[h] = [go(rcopy(v, v, zp(d))) for d in (1, 2, 3)]
         s3[h].append(go(rcopy(v, v, sib)))
@@ -453,10 +507,16 @@
         for r in range(p):
             rp[r, p] = jnp.zeros((T, T), F32)
 
-    def solve(h):
+    def solve(g):
         xs = []
+        half = low((128, HW))
         for p in range(PANELS):
-            acc = jnp.concatenate([sfull[p, s, h] for s in range(2)], axis=1)
+            cols = []
+            for s in range(2):
+                a, b = sfull[p, s, 2 * g], sfull[p, s, 2 * g + 1]
+                cols.append(jnp.concatenate(
+                    [jnp.where(half, a, swap(b)), jnp.where(half, swap(a), b)], axis=0))
+            acc = jnp.concatenate(cols, axis=1)
             for q in range(p):
                 acc = acc - dot3((uth[BLK[q, p]], utl[BLK[q, p]]), xs[q])
             got = dot3((wh_ref[p], wl_ref[p]), split(acc))
@@ -471,61 +531,76 @@
                     which = jnp.where(hit, m, which)
                     is_panel = jnp.where(hit, 1, is_panel)
                 mask = jnp.full((T, HW), is_panel, jnp.int32) == 1
-                at = s * T + h * HW
+                at = s * T + g * HW
                 out_ref[p * T:(p + 1) * T, at:at + HW] = jnp.where(
-                    mask, rp[which, p, :, h * HW:(h + 1) * HW], got[:, s * HW:(s + 1) * HW])
-
+                    mask, rp[which, p, :, g * HW:(g + 1) * HW], got[:, s * HW:(s + 1) * HW])
+
+    def solved(g):
+        for h in (2 * g, 2 * g + 1):
+            for c in s3[h][3:]:
+                c.wait_recv()
+        solve(g)
+
+    start_p()
+    start_near(0, 0)
+    gram()
+    sum0()
+    start_near(0, 1)
+    sum1()
+    start_near(1, 0)
+    start_near(1, 1)
+    start_sib(1)
+    start_sib(0)
+    forward_a(0)
+    forward_p()
+    pack(2)
+    pack(3)
+    start_sib(3)
+    forward_a(1)
+    start_near(3, 0)
+    sum2()
+    sib_a(1)
+    sib_a(0)
+    finish_a(0)
+    sum3()
+    ready_p()
     products(0)
-    forward_a(1)
-    for c in g3:
-        c.wait_recv()
-    fa = pl.multiple_of(my_a + y * GS, GS)
-    fb = pl.multiple_of(my_b + x * GS, GS)
-    gfin_a = gza[0] + gza[1] + gza[2] + gza[3]
-    gfin_b = gzb[0] + gzb[1] + gzb[2] + gzb[3]
-    cw[pl.ds(fa, GS), :] = gfin_a
-    cw[pl.ds(fb, GS), :] = gfin_b
-    g4 = []
-    for d in (1, 2, 3):
-        v = cw.at[pl.ds(fa, GS)]
-        g4.append(go(rcopy(v, v, yp(d))))
-        v = cw.at[pl.ds(fb, GS)]
-        g4.append(go(rcopy(v, v, xp(d))))
-    sib_a(1)
+    start_near(2, 0)
+    start_near(2, 1)
+    start_near(3, 1)
+    finish_a(1)
+    back4()
+    products(1)
+    forward_a(2)
     reduce2(0)
-    finish_a(1)
-    for c in g4:
-        c.wait_recv()
-    g5 = []
-    for d in (1, 2, 3):
-        v = cw.at[pl.ds(my_a, GC)]
-        g5.append(go(rcopy(v, v, xp(d))))
-        v = cw.at[pl.ds(my_b, GC)]
-        g5.append(go(rcopy(v, v, yp(d))))
-    products(1)
+    forward_a(3)
+    start_sib(2)
+    back5()
+    sib_a(2)
+    reduce2(1)
+    sib_a(3)
+    finish_a(2)
+    finish_a(3)
+    products(2)
     gather1(0)
-    for c in g5:
-        c.wait_recv()
-    v = cw.at[pl.ds(gk, GHALF)]
-    g6 = go(rcopy(v, v, sib))
+    back6()
+    products(3)
+    gather1(1)
+    gram_back()
+    factor(0)
+    reduce2(2)
+    factor(1)
+    reduce2(3)
+    gather2(1)
+    gather1(2)
+    factor(2)
     gather2(0)
-    g6.wait_recv()
-    for c in g4 + g5 + [g6]:
-        c.wait_send()
-        left_early.append(id(c))
-    factor(0)
-    factor(1)
-    reduce2(1)
-    factor(2)
-    gather1(1)
+    gather1(3)
     factor(3)
-    for c in s3[0][3:]:
-        c.wait_recv()
-    solve(0)
-    gather2(1)
-    for c in s3[1][3:]:
-        c.wait_recv()
-    solve(1)
+    solved(0)
+    gather2(2)
+    gather2(3)
+    solved(1)
     good = checks[0]
     for c in checks[1:]:
         good = jnp.logical_and(good, c)
@@ -538,7 +613,7 @@
 
 
 def fast(child_blocks, home_child, col_tiles, tile_owner):
-    sem = SEM_FIX + 48
+    sem = SEM_FIX + 24 * H
     vm = pltpu.VMEM
     vmem = pl.BlockSpec(memory_space=pltpu.VMEM)
     smem = pl.BlockSpec(memory_space=pltpu.SMEM)
@@ -551,25 +626,25 @@
         in_specs=[smem, smem, smem, vmem],
         out_specs=(vmem, smem),
         scratch_shapes=[
-            vm((4, 2, H, OWN * ROWS, REST * HW), F32),
+            vm((4, 2, H, OWN * ROWS, REST * QW), F32),
             vm((PANELS, OWN * ROWS, T), F32),
             vm((4, 2, OWN * ROWS, T), F32),
             vm((4, 2, 8, 128), jnp.int32),
             pltpu.SMEM((4, 2, 8, 128), jnp.int32),
-            vm((REST + 1, 8 * 128, HW), BF),
-            vm((REST + 1, 8 * 128, HW), BF),
+            vm((REST + 2, 8 * 128, HW), BF),
+            vm((REST + 2, 8 * 128, HW), BF),
             vm((T, 1024), BF),
             vm((T, 1024), BF),
             vm((1024, T), BF),
             vm((1024, T), BF),
-            vm((H, 4, 4, T, HW), F32),
             vm((H, 4, 4, 128, HW), F32),
-            vm((H, 4, 4, 128, HW), F32),
-            vm((H, 4, 128, HW), F32),
-            vm((H, 4, 128, HW), F32),
-            vm((H, 3, 128, HW), F32),
-            vm((H, 3, 128, HW), F32),
-            vm((4, 2, H, T, HW), F32),
+            vm((H, 4, 4, 64, HW), F32),
+            vm((H, 4, 4, 64, HW), F32),
+            vm((H, 4, 64, HW), F32),
+            vm((H, 4, 64, HW), F32),
+            vm((H, 3, 64, HW), F32),
+            vm((H, 3, 64, HW), F32),
+            vm((4, 2, H, 128, HW), F32),
             vm((GROWS, T), F32),
             vm((GHALF, T), F32),
             vm((3, GC, T), F32),

time: 106 us -> 98.9 us (0.933)
  Pallas kernels: 99.7 us -> 93.2 us
    pallas_call x1, Pallas kernels: 99.7 us -> 93.2 us  [fast(): pl.pallas_call(kernel, out_shape=(jax.ShapeDtypeStruct((PANELS * T, 2 * T...]
where the time goes in v4:
time: 98.9 us; the launch traced here: 98.7 us
  Pallas kernels  93.2 us (94%)
  local copies, waits for them, and re-layouts  4.58 us (5%)
    pallas_call x1, Pallas kernels, fast(): pl.pallas_call(kernel, out_shape=(jax.ShapeDtypeStruct((PANELS * T, 2 * T...  93.2 us
    unnamed x10, local copies, waits for them, and re-layouts  4.58 us

profile of v4, /device:TPU:1, one launch (start us, length us, event | category | flops | bytes accessed | tf_op | source)
XLA Modules:
  0.0 98.7 jit_solution(9705997291139447179)
XLA Ops:
  0.0 1.5 %copy.73.tiles_ref = s32[256,12]{1,0:T(8,128)} copy(s32[256,12]{0,1:T(8,128)} %param.11) | data formatting | bytes 24576 | tf_op args[2]
  1.5 0.0 copy-start.13
  1.5 0.0 copy-start.20
  1.5 0.0 copy-start.21
  1.5 0.0 copy-start.22
  1.5 93.2 %front.1 = (f32[1024,512]{1,0:T(8,128)}, s32[1]{0:T(128)}) custom-call(s32[2]{0:T(128)} %home_ref.1, s32[256,12]{1,0:T(8,128)} %copy.73.tiles_ref, s32[32]{0:T(128)} %owner_ref.1, f32[2,64,3072]{2,1,0:T(8,128)} %blocks_ref.1), custom_call_target="tpu_custom_call" | custom-call | flops 10000000000 | bytes 10000000 | tf_op jit(solution)/shard_map/front/pallas_call | solution.py:620
  95.3 0.0 copy-done.13
  95.3 0.0 copy-done.20
  95.3 0.0 copy-done.21
  95.4 0.0 copy-done.22
  95.4 0.3 conditional.1
  95.6 3.1 %copy.128 = f32[1024,512]{1,0:T(8,128)} copy(f32[1024,512]{1,0:T(8,128)} %get-tuple-element.27) | data formatting | bytes 4194304
Async XLA Ops:
  1.5 93.8 %copy-start.13 = (f32[2,64,3072]{2,1,0:T(8,128)S(1)}, f32[2,64,3072]{2,1,0:T(8,128)}, u32[]{:S(2)}) copy-start(f32[2,64,3072]{2,1,0:T(8,128)} %blocks_ref.1) | copy-start | bytes 4718596
  1.5 93.9 %copy-start.20 = (s32[256,12]{0,1:T(8,128)S(1)}, s32[256,12]{0,1:T(8,128)}, u32[]{:S(2)}) copy-start(s32[256,12]{0,1:T(8,128)} %param.11) | copy-start | bytes 36868
  1.5 93.9 %copy-start.21 = (s32[32]{0:T(128)S(1)}, s32[32]{0:T(128)}, u32[]{:S(2)}) copy-start(s32[32]{0:T(128)} %owner_ref.1) | copy-start | bytes 388
  1.5 93.9 %copy-start.22 = (s32[2]{0:T(128)S(1)}, s32[2]{0:T(128)}, u32[]{:S(2)}) copy-start(s32[2]{0:T(128)} %home_ref.1) | copy-start | bytes 28

commit v5 on v4

--- a/solution.py
+++ b/solution.py
@@ -107,7 +107,7 @@
         rest_at = [jnp.int32(0)] * REST
         count = jnp.int32(0)
         for j in range(CT):
-            t = tiles_ref[home, j]
+            t = tiles_ref[j, home]
             p = owner_ref[t]
             rest = t >= PANELS
             for m in range(PANELS):
@@ -314,7 +314,7 @@
             agh[REST + i] = zero
             agl[REST + i] = zero
 
-    def products(h):
+    def convert(h):
         for c in asib[h]:
             c.wait_recv()
 
@@ -330,46 +330,48 @@
 
         lax.fori_loop(0, 8, conv, 0)
 
-        for part in range(2):
-            j = x // 2 if part else 1 - x // 2
-
-            def pair(b, carry, part=part, j=j):
-                mask = low((ROWS, HW))
-                rows_at = [lax.rem(y + 1 + 2 * b + u, 4) for u in range(2)]
-                for u in range(2):
-                    slot = (rows_at[u] * 4 + 2 * j) * 2 + k
-                    for n in range(16):
-                        at0 = tab_s[n // 4, (n // 2) % 2, n % 2, slot]
-                        at1 = tab_s[n // 4, (n // 2) % 2, n % 2, slot + 2]
-                        at1 = at1 + 1 - 2 * lax.rem(at1, 2)
-                        rn = slice(n * ROWS, (n + 1) * ROWS)
-                        cn = slice(u * HW, (u + 1) * HW)
-                        bh[rn, cn] = jnp.where(mask, agh[at0, rn, :], agh[at1, rn, :])
-                        bl[rn, cn] = jnp.where(mask, agl[at0, rn, :], agl[at1, rn, :])
-                got = dot3((pth[...], ptl[...]), (bh[...], bl[...]))
-                half = low((128, HW))
-                for u in range(2):
-                    top = got[0:128, u * HW:(u + 1) * HW]
-                    bottom = got[128:256, u * HW:(u + 1) * HW]
-                    yy = rows_at[u]
-                    sp[h, yy, 2 * j] = jnp.where(half, top, swap(bottom))
-                    sp[h, yy, 2 * j + 1] = jnp.where(half, swap(top), bottom)
-                for u in range(2):
-                    yy = rows_at[u]
-                    if part:
-                        first(h, 2 * j + 1 - lax.rem(x, 2), yy).start()
-                    else:
-                        first(h, 2 * j, yy).start()
-                        first(h, 2 * j + 1, yy).start()
-                second(h, rows_at[0], j).start()
-
-                @pl.when(b == 0)
-                def _():
-                    second(h, rows_at[1], j).start()
-
-                return carry
-
-            lax.fori_loop(0, 2, pair, 0)
+    def products(h, part):
+        if part == 0:
+            convert(h)
+        j = x // 2 if part else 1 - x // 2
+
+        def pair(b, carry):
+            mask = low((ROWS, HW))
+            rows_at = [lax.rem(y + 1 + 2 * b + u, 4) for u in range(2)]
+            for u in range(2):
+                slot = (rows_at[u] * 4 + 2 * j) * 2 + k
+                for n in range(16):
+                    at0 = tab_s[n // 4, (n // 2) % 2, n % 2, slot]
+                    at1 = tab_s[n // 4, (n // 2) % 2, n % 2, slot + 2]
+                    at1 = at1 + 1 - 2 * lax.rem(at1, 2)
+                    rn = slice(n * ROWS, (n + 1) * ROWS)
+                    cn = slice(u * HW, (u + 1) * HW)
+                    bh[rn, cn] = jnp.where(mask, agh[at0, rn, :], agh[at1, rn, :])
+                    bl[rn, cn] = jnp.where(mask, agl[at0, rn, :], agl[at1, rn, :])
+            got = dot3((pth[...], ptl[...]), (bh[...], bl[...]))
+            half = low((128, HW))
+            for u in range(2):
+                top = got[0:128, u * HW:(u + 1) * HW]
+                bottom = got[128:256, u * HW:(u + 1) * HW]
+                yy = rows_at[u]
+                sp[h, yy, 2 * j] = jnp.where(half, top, swap(bottom))
+                sp[h, yy, 2 * j + 1] = jnp.where(half, swap(top), bottom)
+            for u in range(2):
+                yy = rows_at[u]
+                if part:
+                    first(h, 2 * j + 1 - lax.rem(x, 2), yy).start()
+                else:
+                    first(h, 2 * j, yy).start()
+                    first(h, 2 * j + 1, yy).start()
+            second(h, rows_at[0], j).start()
+
+            @pl.when(b == 0)
+            def _():
+                second(h, rows_at[1], j).start()
+
+            return carry
+
+        lax.fori_loop(0, 2, pair, 0)
 
     base1 = SEM_FIX
 
@@ -541,60 +543,64 @@
                 c.wait_recv()
         solve(g)
 
+    start_near(0, 0)
+    start_sib(1)
     start_p()
-    start_near(0, 0)
     gram()
+    start_sib(0)
     sum0()
+    start_near(1, 0)
     start_near(0, 1)
+    pack(3)
+    forward_a(0)
     sum1()
-    start_near(1, 0)
+    pack(2)
     start_near(1, 1)
-    start_sib(1)
-    start_sib(0)
-    forward_a(0)
     forward_p()
-    pack(2)
-    pack(3)
-    start_sib(3)
     forward_a(1)
+    start_sib(2)
+    start_near(2, 0)
     start_near(3, 0)
     sum2()
-    sib_a(1)
     sib_a(0)
     finish_a(0)
+    ready_p()
+    products(0, 0)
+    sib_a(1)
+    products(0, 1)
+    finish_a(1)
     sum3()
-    ready_p()
-    products(0)
-    start_near(2, 0)
     start_near(2, 1)
-    start_near(3, 1)
-    finish_a(1)
+    products(1, 0)
+    start_sib(3)
+    products(1, 1)
     back4()
-    products(1)
     forward_a(2)
     reduce2(0)
+    start_near(3, 1)
+    reduce2(1)
+    back5()
     forward_a(3)
-    start_sib(2)
-    back5()
     sib_a(2)
-    reduce2(1)
+    finish_a(2)
     sib_a(3)
-    finish_a(2)
+    products(2, 0)
     finish_a(3)
-    products(2)
+    products(2, 1)
+    products(3, 0)
     gather1(0)
     back6()
-    products(3)
-    gather1(1)
+    products(3, 1)
     gram_back()
     factor(0)
+    gather1(1)
     reduce2(2)
     factor(1)
     reduce2(3)
-    gather2(1)
+    gather2(0)
     gather1(2)
     factor(2)
-    gather2(0)
+    gather2(1)
     gather1(3)
     factor(3)
     solved(0)
@@ -671,7 +677,7 @@
         ),
         cost_estimate=pl.CostEstimate(flops=10**10, bytes_accessed=10**7, transcendentals=0),
         name="front",
-    )(home_child, col_tiles, tile_owner, child_blocks)
+    )(home_child, col_tiles.T, tile_owner, child_blocks)
 
 
 def total(x, axis):

time: 98.9 us -> 93.9 us (0.949)
  Pallas kernels: 93.2 us -> 89.7 us
  local copies, waits for them, and re-layouts: 4.58 us -> 3.1 us
    pallas_call x1, Pallas kernels: 93.2 us -> 89.7 us  [fast(): pl.pallas_call(kernel, out_shape=(jax.ShapeDtypeStruct((PANELS * T, 2 * T...]
    unnamed x10 -> x9, local copies, waits for them, and re-layouts: 4.58 us -> 3.1 us
where the time goes in v5:
time: 93.9 us; the launch traced here: 93.7 us
  Pallas kernels  89.7 us (96%)
  local copies, waits for them, and re-layouts  3.1 us (3%)
    pallas_call x1, Pallas kernels, fast(): pl.pallas_call(kernel, out_shape=(jax.ShapeDtypeStruct((PANELS * T, 2 * T...  89.7 us
    unnamed x9, local copies, waits for them, and re-layouts  3.1 us

profile of v5, /device:TPU:1, one launch (start us, length us, event | category | flops | bytes accessed | tf_op | source)
XLA Modules:
  0.0 93.7 jit_solution(5498541690486469077)
XLA Ops:
  0.0 0.0 copy-start.13
  0.0 0.0 copy-start.20
  0.0 0.0 copy-start.21
  0.0 0.0 copy-start.22
  0.0 89.7 %front.1 = (f32[1024,512]{1,0:T(8,128)}, s32[1]{0:T(128)}) custom-call(s32[2]{0:T(128)} %home_ref.1, s32[12,256]{1,0:T(8,128)} %bitcast.172, s32[32]{0:T(128)} %owner_ref.1, f32[2,64,3072]{2,1,0:T(8,128)} %blocks_ref.1), custom_call_target="tpu_custom_call" | custom-call | flops 10000000000 | bytes 10000000 | tf_op jit(solution)/shard_map/front/pallas_call | solution.py:626
  90.3 0.0 copy-done.13
  90.3 0.0 copy-done.20
  90.3 0.0 copy-done.21
  90.4 0.0 copy-done.22
  90.4 0.3 conditional.1
  90.6 3.1 %copy.124 = f32[1024,512]{1,0:T(8,128)} copy(f32[1024,512]{1,0:T(8,128)} %get-tuple-element.27) | data formatting | bytes 4194304
Async XLA Ops:
  0.0 90.3 %copy-start.13 = (f32[2,64,3072]{2,1,0:T(8,128)S(1)}, f32[2,64,3072]{2,1,0:T(8,128)}, u32[]{:S(2)}) copy-start(f32[2,64,3072]{2,1,0:T(8,128)} %blocks_ref.1) | copy-start | bytes 4718596
  0.0 90.3 %copy-start.20 = (s32[256,12]{0,1:T(8,128)S(1)}, s32[256,12]{0,1:T(8,128)}, u32[]{:S(2)}) copy-start(s32[256,12]{0,1:T(8,128)} %param.11) | copy-start | bytes 36868
  0.0 90.3 %copy-start.21 = (s32[32]{0:T(128)S(1)}, s32[32]{0:T(128)}, u32[]{:S(2)}) copy-start(s32[32]{0:T(128)} %owner_ref.1) | copy-start | bytes 388
  0.0 90.3 %copy-start.22 = (s32[2]{0:T(128)S(1)}, s32[2]{0:T(128)}, u32[]{:S(2)}) copy-start(s32[2]{0:T(128)} %home_ref.1) | copy-start | bytes 28

commit v6 on v5

--- a/solution.py
+++ b/solution.py
@@ -626,7 +626,7 @@
     return pl.pallas_call(
         kernel,
         out_shape=(
-            jax.ShapeDtypeStruct((PANELS * T, 2 * T), F32),
+            pltpu.VMEM((PANELS * T, 2 * T), F32),
             jax.ShapeDtypeStruct((1,), jnp.int32),
         ),
         in_specs=[smem, smem, smem, vmem],
@@ -673,7 +673,7 @@
             pltpu.SemaphoreType.DMA((1,)),
         ],
         compiler_params=pltpu.CompilerParams(
-            collective_id=0, has_side_effects=True, vmem_limit_bytes=60 * 1024 * 1024
+            collective_id=0, has_side_effects=True, vmem_limit_bytes=52 * 1024 * 1024
         ),
         cost_estimate=pl.CostEstimate(flops=10**10, bytes_accessed=10**7, transcendentals=0),
         name="front",

time: 93.9 us -> 91.1 us (0.970)
  local copies, waits for them, and re-layouts: 3.1 us -> 1.33 us
  Pallas kernels: 89.7 us -> 88.7 us
    unnamed x9 -> x7, local copies, waits for them, and re-layouts: 3.1 us -> 1.33 us
    pallas_call x1, Pallas kernels: 89.7 us -> 88.7 us  [fast(): pl.pallas_call(kernel, out_shape=(pltpu.VMEM((PANELS * T, 2 * T), F32), j...]
where the time goes in v6:
time: 91.1 us; the launch traced here: 91 us
  Pallas kernels  88.7 us (97%)
  local copies, waits for them, and re-layouts  1.33 us (1%)
    pallas_call x1, Pallas kernels, fast(): pl.pallas_call(kernel, out_shape=(pltpu.VMEM((PANELS * T, 2 * T), F32), j...  88.7 us

profile of v6, /device:TPU:1, one launch (start us, length us, event | category | flops | bytes accessed | tf_op | source)
XLA Modules:
  0.0 91.0 jit_solution(3145822892335899498)
XLA Ops:
  0.0 0.0 copy-start.13
  0.0 0.0 copy-start.14
  0.0 0.0 copy-start.15
  0.0 88.7 %front.1 = (f32[1024,512]{1,0:T(8,128)S(1)}, s32[1]{0:T(128)}) custom-call(s32[2]{0:T(128)} %home_ref.1, s32[12,256]{1,0:T(8,128)} %bitcast.172, s32[32]{0:T(128)} %owner_ref.1, f32[2,64,3072]{2,1,0:T(8,128)} %blocks_ref.1), custom_call_target="tpu_custom_call" | custom-call | flops 10000000000 | bytes 10000000 | tf_op jit(solution)/shard_map/front/pallas_call | solution.py:626
  89.4 0.0 copy-done.13
  89.4 0.0 copy-done.14
  89.4 0.0 copy-done.15
  89.4 0.3 conditional.1
  89.7 1.3 %copy.119 = f32[1024,512]{1,0:T(8,128)} copy(f32[1024,512]{1,0:T(8,128)S(1)} %get-tuple-element.27) | data formatting | bytes 4194304
Async XLA Ops:
  0.0 89.4 %copy-start.13 = (s32[256,12]{0,1:T(8,128)S(1)}, s32[256,12]{0,1:T(8,128)}, u32[]{:S(2)}) copy-start(s32[256,12]{0,1:T(8,128)} %param.11) | copy-start | bytes 36868
  0.0 89.4 %copy-start.14 = (s32[32]{0:T(128)S(1)}, s32[32]{0:T(128)}, u32[]{:S(2)}) copy-start(s32[32]{0:T(128)} %owner_ref.1) | copy-start | bytes 388
  0.0 89.4 %copy-start.15 = (s32[2]{0:T(128)S(1)}, s32[2]{0:T(128)}, u32[]{:S(2)}) copy-start(s32[2]{0:T(128)} %home_ref.1) | copy-start | bytes 28

commit v7 on v6

--- a/solution.py
+++ b/solution.py
@@ -544,63 +544,63 @@
         solve(g)
 
     start_near(0, 0)
-    start_sib(1)
+    gram()
+    sum0()
     start_p()
-    gram()
+    start_near(1, 0)
+    sum1()
     start_sib(0)
-    sum0()
-    start_near(1, 0)
     start_near(0, 1)
-    pack(3)
+    pack(2)
     forward_a(0)
-    sum1()
-    pack(2)
     start_near(1, 1)
     forward_p()
     forward_a(1)
+    sum2()
+    ready_p()
+    pack(3)
+    sib_a(0)
+    start_sib(1)
+    finish_a(0)
+    sib_a(1)
+    sum3()
+    products(0, 0)
     start_sib(2)
+    start_sib(3)
+    start_near(3, 0)
     start_near(2, 0)
-    start_near(3, 0)
-    sum2()
-    sib_a(0)
-    finish_a(0)
-    ready_p()
-    products(0, 0)
-    sib_a(1)
+    start_near(3, 1)
     products(0, 1)
     finish_a(1)
-    sum3()
     start_near(2, 1)
+    back4()
     products(1, 0)
-    start_sib(3)
     products(1, 1)
-    back4()
+    reduce2(0)
+    back5()
     forward_a(2)
-    reduce2(0)
-    start_near(3, 1)
+    forward_a(3)
+    sib_a(3)
     reduce2(1)
-    back5()
-    forward_a(3)
     sib_a(2)
     finish_a(2)
-    sib_a(3)
     products(2, 0)
+    gather1(0)
     finish_a(3)
     products(2, 1)
+    back6()
     products(3, 0)
-    gather1(0)
-    back6()
+    gather1(1)
     products(3, 1)
     gram_back()
     factor(0)
-    gather1(1)
     reduce2(2)
     factor(1)
+    gather2(0)
     reduce2(3)
-    gather2(0)
+    gather2(1)
     gather1(2)
     factor(2)
-    gather2(1)
     gather1(3)
     factor(3)
     solved(0)

time: 91.1 us -> 91.3 us (level)
  no operation moved by 1% of the time
where the time goes in v7:
time: 91.3 us; the launch traced here: 91.1 us
  Pallas kernels  88.8 us (97%)
  local copies, waits for them, and re-layouts  1.33 us (1%)
    pallas_call x1, Pallas kernels, fast(): pl.pallas_call(kernel, out_shape=(pltpu.VMEM((PANELS * T, 2 * T), F32), j...  88.8 us

profile of v7, /device:TPU:1, one launch (start us, length us, event | category | flops | bytes accessed | tf_op | source)
XLA Modules:
  0.0 91.1 jit_solution(4699655760534877921)
XLA Ops:
  0.0 0.0 copy-start.13
  0.0 0.0 copy-start.14
  0.0 0.0 copy-start.15
  0.0 88.8 %front.1 = (f32[1024,512]{1,0:T(8,128)S(1)}, s32[1]{0:T(128)}) custom-call(s32[2]{0:T(128)} %home_ref.1, s32[12,256]{1,0:T(8,128)} %bitcast.172, s32[32]{0:T(128)} %owner_ref.1, f32[2,64,3072]{2,1,0:T(8,128)} %blocks_ref.1), custom_call_target="tpu_custom_call" | custom-call | flops 10000000000 | bytes 10000000 | tf_op jit(solution)/shard_map/front/pallas_call | solution.py:626
  89.5 0.0 copy-done.13
  89.5 0.0 copy-done.14
  89.5 0.0 copy-done.15
  89.5 0.3 conditional.1
  89.8 1.3 %copy.119 = f32[1024,512]{1,0:T(8,128)} copy(f32[1024,512]{1,0:T(8,128)S(1)} %get-tuple-element.27) | data formatting | bytes 4194304
Async XLA Ops:
  0.0 89.5 %copy-start.13 = (s32[256,12]{0,1:T(8,128)S(1)}, s32[256,12]{0,1:T(8,128)}, u32[]{:S(2)}) copy-start(s32[256,12]{0,1:T(8,128)} %param.11) | copy-start | bytes 36868
  0.0 89.5 %copy-start.14 = (s32[32]{0:T(128)S(1)}, s32[32]{0:T(128)}, u32[]{:S(2)}) copy-start(s32[32]{0:T(128)} %owner_ref.1) | copy-start | bytes 388
  0.0 89.5 %copy-start.15 = (s32[2]{0:T(128)S(1)}, s32[2]{0:T(128)}, u32[]{:S(2)}) copy-start(s32[2]{0:T(128)} %home_ref.1) | copy-start | bytes 28
